TPU v7x, 32 devices: a whole 2x2x4 slice. The times are simulated.
32 devices in a mesh: line: 4 (over x, core), dp: 8 (over z, y).
Axes of the slice: x: 2, y: 2, z: 4, core: 2. Of those that a mesh axis runs over, the one named last changes fastest.
Arguments:
- fields: bfloat16 [8, 2048, 128], P('dp', 'line'), may hold values from -6 to 6
- cotangent: bfloat16 [8, 2048, 128], P('dp', 'line'), may hold values from -6 to 6
- norm_gain: float32 [3, 128], replicated, may hold values from 0.1 to 1.9
- kernel: float32 [3, 15, 128], replicated, may hold values from -1.8 to 1.8
- mix_weight: bfloat16 [3, 128, 128], replicated, may hold values from -0.5 to 0.5
- line_order: int32 [3, 2048], P(None, 'line'), may hold values from 0 to 511, as said below
- line_starts: int32 [3, 16], P(None, 'line'), may hold values from 0 to 32
Outputs:
- imitated: bfloat16 [8, 2048, 128], P('dp', 'line')
- field_grad: bfloat16 [8, 2048, 128], P('dp', 'line')
- mix_grad: float32 [3, 128, 128], replicated
- kernel_grad: float32 [3, 15, 128], replicated
- gain_grad: float32 [3, 128], replicated
Inputs may be any that keep to these rules, and one draw needn't show every extreme that they name: For each direction, every aligned block of 512 entries of line_order is a permutation of 0 to 511.
All inputs are finite; a program needn't handle non-finite values.
Results may differ from a plain program's by a relative error of at most 0.014.
Values may be sent and summed in bfloat16 or wider, within the bound.
A program may use at most 64 MiB of HBM per device.

v0:
```python
import jax
import jax.numpy as jnp
from jax import lax
from jax.sharding import PartitionSpec as P

LINE = 128


EPSILON = 1e-06


def tap_offsets():
    offsets = [0]
    for dilation_level in range(7):
        offsets = offsets + [-(2**dilation_level), 2**dilation_level]
    return offsets


def shifted(values, offset):
    if offset > 0:
        return jnp.concatenate([values[:, offset:], jnp.zeros_like(values[:, :offset])], axis=1)
    if offset < 0:
        return jnp.concatenate([jnp.zeros_like(values[:, offset:]), values[:, :offset]], axis=1)
    return values


def depthwise(inputs, weights):
    running = jnp.zeros(inputs.shape, jnp.float32)
    for tap_index, offset in enumerate(tap_offsets()):
        running = running + weights[tap_index] * shifted(inputs, offset)
    return running


def depthwise_transpose(grads, weights):
    running = jnp.zeros(grads.shape, jnp.float32)
    for tap_index, offset in enumerate(tap_offsets()):
        running = running + weights[tap_index] * shifted(grads, -offset)
    return running


def kernel_terms(grads, inputs):
    return jnp.stack(
        [jnp.sum(grads * shifted(inputs, offset), axis=(0, 1)) for offset in tap_offsets()]
    )


def block_view(array, line_count):
    batch_len, cell_count, channels = array.shape
    return array.reshape(batch_len, line_count, cell_count // line_count, channels)


def unpermute(array, table):
    return jnp.zeros_like(array).at[:, table].set(array)


def into_lines(array, table, shift, line_count):
    rolled = jnp.roll(block_view(array, line_count), shift, axis=1).reshape(array.shape)
    received = lax.all_to_all(rolled, "line", split_axis=1, concat_axis=1, tiled=True)
    return jnp.take(received, table, axis=1)


def out_of_lines(array, table, shift, line_count):
    placed = unpermute(array, table)
    received = lax.all_to_all(placed, "line", split_axis=1, concat_axis=1, tiled=True)
    return jnp.roll(block_view(received, line_count), -shift, axis=1).reshape(array.shape)


def advance(array, table_now, table_next, line_rank, line_count):
    placed = unpermute(array, table_now)
    rolled = jnp.roll(block_view(placed, line_count), line_rank, axis=1).reshape(array.shape)
    received = lax.all_to_all(rolled, "line", split_axis=1, concat_axis=1, tiled=True)
    order_index = (line_rank - jnp.arange(line_count, dtype=jnp.int32)) % line_count
    reordered = jnp.take(block_view(received, line_count), order_index, axis=1).reshape(array.shape)
    return jnp.take(reordered, table_next, axis=1)


def retreat(array, table_now, table_prev, line_rank, line_count):
    placed = unpermute(array, table_now)
    order_index = (line_rank - jnp.arange(line_count, dtype=jnp.int32)) % line_count
    reordered = jnp.take(block_view(placed, line_count), order_index, axis=1).reshape(array.shape)
    received = lax.all_to_all(reordered, "line", split_axis=1, concat_axis=1, tiled=True)
    rolled = jnp.roll(block_view(received, line_count), -line_rank, axis=1).reshape(array.shape)
    return jnp.take(rolled, table_prev, axis=1)


def norm_forward(stream, gain_row):
    values = stream.astype(jnp.float32)
    inverse = lax.rsqrt(jnp.mean(values * values, axis=-1, keepdims=True) + EPSILON)
    scaled = values * inverse
    normed = (scaled * gain_row).astype(jnp.bfloat16)
    return (values, inverse, scaled, normed)


def norm_backward(grad_cells, inverse, scaled, gain_row, grad_stream):
    cells_f = grad_cells.astype(jnp.float32)
    gain_part = jnp.sum(cells_f * scaled, axis=(0, 1))
    weighted = cells_f * gain_row
    grad_norm = inverse * (weighted - scaled * jnp.mean(weighted * scaled, axis=-1, keepdims=True))
    return (gain_part, (grad_stream.astype(jnp.float32) + grad_norm).astype(jnp.bfloat16))


def line_forward(regrouped, keep_mask, weights, mixing):
    channels = regrouped.shape[2]
    lined = regrouped.reshape(-1, LINE, channels)
    masked = jnp.where(keep_mask[:, :, None], lined, jnp.zeros_like(lined))
    hidden = depthwise(masked.astype(jnp.float32), weights)
    activated = jax.nn.silu(hidden).astype(jnp.bfloat16)
    mixed = jnp.dot(
        activated.reshape(-1, channels), mixing, preferred_element_type=jnp.float32
    ).astype(jnp.bfloat16)
    return (masked, hidden, activated, mixed.reshape(regrouped.shape))


def line_backward(grad_mixed, masked, hidden, activated, keep_mask, weights, mixing):
    channels = grad_mixed.shape[2]
    flat_grad = grad_mixed.reshape(-1, channels)
    mix_part = jnp.einsum(
        "nc,nd->cd", activated.reshape(-1, channels), flat_grad, preferred_element_type=jnp.float32
    )
    grad_act = jnp.einsum(
        "nd,cd->nc", flat_grad, mixing, preferred_element_type=jnp.float32
    ).reshape(hidden.shape)
    gate_value = jax.nn.sigmoid(hidden)
    grad_hidden = (grad_act * (gate_value * (1.0 + hidden * (1.0 - gate_value)))).astype(
        jnp.bfloat16
    )
    hidden_grad_f = grad_hidden.astype(jnp.float32)
    kernel_part = kernel_terms(hidden_grad_f, masked.astype(jnp.float32))
    grad_masked = depthwise_transpose(hidden_grad_f, weights)
    grad_normed = jnp.where(keep_mask[:, :, None], grad_masked, jnp.zeros_like(grad_masked)).astype(
        jnp.bfloat16
    )
    return (mix_part, kernel_part, grad_normed.reshape(grad_mixed.shape))


def body(fields, cotangent, norm_gain, kernel, mix_weight, line_order, line_starts):
    line_count = lax.axis_size("line")
    line_rank = lax.axis_index("line")
    batch_len = fields.shape[0]
    cell_count = fields.shape[1]
    positions = jnp.arange(LINE, dtype=jnp.int32)
    masks = [
        jnp.tile(positions[None, :] >= line_starts[direction][:, None], (batch_len, 1))
        for direction in range(3)
    ]
    grad_scale = float(lax.axis_size("dp") * batch_len * line_count * cell_count) ** (-0.5)
    collected = []

    def collect(mix_part, kernel_part, gain_part):
        collected.append((mix_part, kernel_part, gain_part))

    saved = []
    stream = into_lines(fields, line_order[0], 0, line_count)
    for direction in range(3):
        values, inverse, scaled, normed = norm_forward(stream, norm_gain[direction])
        masked, hidden, activated, mixed = line_forward(
            normed, masks[direction], kernel[direction], mix_weight[direction]
        )
        saved.append((inverse, scaled, masked, hidden, activated))
        stream = (values + mixed.astype(jnp.float32)).astype(jnp.bfloat16)
        if direction < 2:
            stream = advance(
                stream, line_order[direction], line_order[direction + 1], line_rank, line_count
            )
    imitated = out_of_lines(stream, line_order[2], 2 * line_rank, line_count)
    grad_stream = into_lines(cotangent, line_order[2], 2 * line_rank, line_count)
    for direction in (2, 1, 0):
        inverse, scaled, masked, hidden, activated = saved[direction]
        mix_part, kernel_part, grad_normed = line_backward(
            grad_stream,
            masked,
            hidden,
            activated,
            masks[direction],
            kernel[direction],
            mix_weight[direction],
        )
        gain_part, grad_stream = norm_backward(
            grad_normed, inverse, scaled, norm_gain[direction], grad_stream
        )
        collect(mix_part, kernel_part, gain_part)
        if direction > 0:
            grad_stream = retreat(
                grad_stream, line_order[direction], line_order[direction - 1], line_rank, line_count
            )
    field_grad = out_of_lines(grad_stream, line_order[0], 0, line_count)
    ordered = collected[::-1]
    mix_stack = jnp.stack([entry[0] for entry in ordered])
    kernel_stack = jnp.stack([entry[1] for entry in ordered])
    gain_stack = jnp.stack([entry[2] for entry in ordered])
    mix_stack, kernel_stack, gain_stack = lax.psum(
        (mix_stack, kernel_stack, gain_stack), ("line", "dp")
    )
    return (
        imitated,
        field_grad,
        mix_stack * grad_scale,
        kernel_stack * grad_scale,
        gain_stack * grad_scale,
    )


def solution(mesh):
    in_specs = (
        P("dp", "line", None),
        P("dp", "line", None),
        P(),
        P(),
        P(),
        P(None, "line"),
        P(None, "line"),
    )
    out_specs = (P("dp", "line", None), P("dp", "line", None), P(), P(), P())
    return jax.shard_map(body, mesh=mesh, in_specs=in_specs, out_specs=out_specs, check_vma=False)
```

profile of v0, /device:TPU:0, one launch (start us, length us, event | category | flops | bytes accessed | tf_op | source)
XLA Modules:
  0.0 275.6 jit_solution(10530651243218102453)
XLA Ops:
  11.0 4.3 %all-to-all-start = ((bf16[4,2,8192]{2,1,0:T(2,128)(2,1)}), bf16[4,2,8192]{2,1,0:T(2,128)(2,1)S(1)}, u32[]{:S(2)}, u32[]{:S(2)}) async-start(bf16[4,2,8192]{2,1,0:T(2,128)(2,1)} %reshape.893), calls=%async_computation | async-start | bytes 262144 | tf_op jit(solution)/shard_map/all_to_all | solution.py:58
  22.1 3.4 %all-to-all-start.4 = ((bf16[4,2,8192]{2,1,0:T(2,128)(2,1)}), bf16[4,2,8192]{2,1,0:T(2,128)(2,1)S(1)}, u32[]{:S(2)}, u32[]{:S(2)}) async-start(bf16[4,2,8192]{2,1,0:T(2,128)(2,1)} %reshape.901), calls=%async_computation.4 | async-start | bytes 262144 | tf_op jit(solution)/shard_map/all_to_all | solution.py:58
  34.4 3.3 %all-to-all-start.1 = ((bf16[4,2,8192]{2,1,0:T(2,128)(2,1)}), bf16[4,2,8192]{2,1,0:T(2,128)(2,1)S(1)}, u32[]{:S(2)}, u32[]{:S(2)}) async-start(bf16[4,2,8192]{2,1,0:T(2,128)(2,1)} %reshape.895), calls=%async_computation.1 | async-start | bytes 262144 | tf_op jit(solution)/shard_map/all_to_all | solution.py:71
  39.2 3.1 %all-to-all-done.1 = bf16[4,2,8192]{2,1,0:T(2,128)(2,1)S(1)} async-done(((bf16[4,2,8192]{2,1,0:T(2,128)(2,1)}), bf16[4,2,8192]{2,1,0:T(2,128)(2,1)S(1)}, u32[]{:S(2)}, u32[]{:S(2)}) %all-to-all-start.1) | async-done | bytes 131104 | tf_op jit(solution)/shard_map/all_to_all | solution.py:71
  49.0 2.1 scatter_custom_fusion.1
  53.5 3.3 %all-to-all-start.2 = ((bf16[4,2,8192]{2,1,0:T(2,128)(2,1)}), bf16[4,2,8192]{2,1,0:T(2,128)(2,1)S(1)}, u32[]{:S(2)}, u32[]{:S(2)}) async-start(bf16[4,2,8192]{2,1,0:T(2,128)(2,1)} %reshape.897), calls=%async_computation.2 | async-start | bytes 262144 | tf_op jit(solution)/shard_map/all_to_all | solution.py:71
  57.0 4.4 %all-to-all-done.2 = bf16[4,2,8192]{2,1,0:T(2,128)(2,1)S(1)} async-done(((bf16[4,2,8192]{2,1,0:T(2,128)(2,1)}), bf16[4,2,8192]{2,1,0:T(2,128)(2,1)S(1)}, u32[]{:S(2)}, u32[]{:S(2)}) %all-to-all-start.2) | async-done | bytes 131104 | tf_op jit(solution)/shard_map/all_to_all | solution.py:71
  73.3 2.5 scatter_custom_fusion.2
  76.9 2.1 reduce.9
  81.3 2.3 select_convert_fusion.2
  85.6 2.2 scatter_custom_fusion.3
  91.1 3.5 %all-to-all-start.5 = ((bf16[4,2,8192]{2,1,0:T(2,128)(2,1)}), bf16[4,2,8192]{2,1,0:T(2,128)(2,1)S(1)}, u32[]{:S(2)}, u32[]{:S(2)}) async-start(bf16[4,2,8192]{2,1,0:T(2,128)(2,1)} %reshape.903), calls=%async_computation.5 | async-start | bytes 262144 | tf_op jit(solution)/shard_map/all_to_all | solution.py:81
  99.2 4.2 %all-to-all-start.3 = ((bf16[4,2,8192]{2,1,0:T(2,128)(2,1)}), bf16[4,2,8192]{2,1,0:T(2,128)(2,1)}, u32[]{:S(2)}, u32[]{:S(2)}) async-start(bf16[4,2,8192]{2,1,0:T(2,128)(2,1)} %reshape.899), calls=%async_computation.3 | async-start | bytes 262144 | tf_op jit(solution)/shard_map/all_to_all | solution.py:64
  106.5 2.9 %fusion.69 = (f32[128]{0:T(128)}, f32[128]{0:T(128)}, f32[128]{0:T(128)}, f32[128]{0:T(128)}, f32[128]{0:T(128)}, /*index=5*/f32[128]{0:T(128)}, f32[128]{0:T(12...) fusion(f32[4,64,128]{2,1,0:T(8,128)} %copy-done.33, ...), kind=kOutput, calls=%fused_computation.139 | convolution fusion | flops 19527808 | bytes 3981312 | tf_op jit(solution)/shard_map/nd,cd->nc/dot_general | solution.py:120
  117.4 2.0 select_convert_fusion.1
  120.7 2.2 scatter_custom_fusion.4
  126.2 3.5 %all-to-all-start.6 = ((bf16[4,2,8192]{2,1,0:T(2,128)(2,1)}), bf16[4,2,8192]{2,1,0:T(2,128)(2,1)S(1)}, u32[]{:S(2)}, u32[]{:S(2)}) async-start(bf16[4,2,8192]{2,1,0:T(2,128)(2,1)} %reshape.905), calls=%async_computation.6 | async-start | bytes 262144 | tf_op jit(solution)/shard_map/all_to_all | solution.py:81
  132.3 1.9 all-to-all-done.6
  137.6 2.3 fusion.67
  148.1 40.5 %all-reduce.84 = (f32[3,15,128]{2,1,0:T(8,128)S(1)}, f32[3,128]{1,0:T(4,128)S(1)}) all-reduce(f32[3,15,128]{2,1,0:T(8,128)S(1)} %pad_maximum_fusion.1, f32[3,128]{1,0:T(4,128)S(1)} %pad_maximum_fusion.2), channel_id=1, replica_groups=mesh['line'=4,'dp'=8] {'line','dp'}, use_global_device_ids=true, to_apply=%region_58.62 | all-reduce | flops 6144 | bytes 49152 | tf_op jit(solution)/shard_map/psum | solution.py:191
  189.2 2.2 scatter_custom_fusion.5
  193.8 3.5 %all-to-all-start.7 = ((bf16[4,2,8192]{2,1,0:T(2,128)(2,1)}), bf16[4,2,8192]{2,1,0:T(2,128)(2,1)S(1)}, u32[]{:S(2)}, u32[]{:S(2)}) async-start(bf16[4,2,8192]{2,1,0:T(2,128)(2,1)} %reshape.907), calls=%async_computation.7 | async-start | bytes 262144 | tf_op jit(solution)/shard_map/all_to_all | solution.py:64
  197.9 4.1 %all-to-all-done.7 = bf16[4,2,8192]{2,1,0:T(2,128)(2,1)S(1)} async-done(((bf16[4,2,8192]{2,1,0:T(2,128)(2,1)}), bf16[4,2,8192]{2,1,0:T(2,128)(2,1)S(1)}, u32[]{:S(2)}, u32[]{:S(2)}) %all-to-all-start.7) | async-done | bytes 131104 | tf_op jit(solution)/shard_map/all_to_all | solution.py:64
  202.8 64.4 %all-reduce.87.cloned.1.call-done = f32[3,128,128]{2,1,0:T(8,128)} async-done(((f32[3,128,128]{2,1,0:T(8,128)}), f32[3,128,128]{2,1,0:T(8,128)}) %all-reduce.87.cloned.1.call-update) | async-done | bytes 196624 | tf_op jit(solution)/shard_map/psum | solution.py:191
  (458 shorter events, 89.0 us)
Async XLA Ops:
  11.0 11.1 %all-to-all-start = ((bf16[4,2,8192]{2,1,0:T(2,128)(2,1)}), bf16[4,2,8192]{2,1,0:T(2,128)(2,1)S(1)}, u32[]{:S(2)}, u32[]{:S(2)}) async-start(bf16[4,2,8192]{2,1,0:T(2,128)(2,1)} %reshape.893), calls=%async_computation | async-start | bytes 262144 | tf_op jit(solution)/shard_map/all_to_all | solution.py:58
  16.0 14.2 %copy-start.96 = (s32[512,1]{0,1:T(1,128)}, s32[512,1]{0,1:T(1,128)S(1)}, u32[]{:S(2)}) copy-start(s32[512,1]{0,1:T(1,128)S(1)} %get-tuple-element.209) | copy-start | bytes 6148
  17.3 10.7 %copy-start.70 = (f32[128]{0:T(128)}, f32[128]{0:T(128)S(1)}, u32[]{:S(2)}) copy-start(f32[128]{0:T(128)S(1)} %get-tuple-element.200) | copy-start | bytes 1540
  17.3 10.7 %copy-start.72 = (f32[128]{0:T(128)}, f32[128]{0:T(128)S(1)}, u32[]{:S(2)}) copy-start(f32[128]{0:T(128)S(1)} %get-tuple-element.201) | copy-start | bytes 1540
  17.3 10.7 %copy-start.74 = (f32[128]{0:T(128)}, f32[128]{0:T(128)S(1)}, u32[]{:S(2)}) copy-start(f32[128]{0:T(128)S(1)} %get-tuple-element.202) | copy-start | bytes 1540
  17.3 10.7 %copy-start.76 = (f32[128]{0:T(128)}, f32[128]{0:T(128)S(1)}, u32[]{:S(2)}) copy-start(f32[128]{0:T(128)S(1)} %get-tuple-element.203) | copy-start | bytes 1540
  17.3 10.7 %copy-start.78 = (f32[128]{0:T(128)}, f32[128]{0:T(128)S(1)}, u32[]{:S(2)}) copy-start(f32[128]{0:T(128)S(1)} %get-tuple-element.204) | copy-start | bytes 1540
  17.3 10.7 %copy-start.80 = (f32[128]{0:T(128)}, f32[128]{0:T(128)S(1)}, u32[]{:S(2)}) copy-start(f32[128]{0:T(128)S(1)} %get-tuple-element.205) | copy-start | bytes 1540
  18.6 9.5 %copy-start.86 = (f32[128]{0:T(128)}, f32[128]{0:T(128)S(1)}, u32[]{:S(2)}) copy-start(f32[128]{0:T(128)S(1)} %get-tuple-element.192) | copy-start | bytes 1540
  19.4 25.4 %copy-start.64 = (f32[128]{0:T(128)}, f32[128]{0:T(128)S(1)}, u32[]{:S(2)}) copy-start(f32[128]{0:T(128)S(1)} %get-tuple-element.217) | copy-start | bytes 1540
  19.4 44.5 %copy-start.66 = (f32[128]{0:T(128)}, f32[128]{0:T(128)S(1)}, u32[]{:S(2)}) copy-start(f32[128]{0:T(128)S(1)} %get-tuple-element.216) | copy-start | bytes 1540
  19.5 42.1 %copy-start.53 = (s32[1024]{0:T(1024)}, s32[1024]{0:T(1024)S(1)}, u32[]{:S(2)}) copy-start(s32[1024]{0:T(1024)S(1)} %pad_clamp_fusion.2) | copy-start | bytes 12292
  19.5 23.6 %copy-start.51 = (s32[1024]{0:T(1024)}, s32[1024]{0:T(1024)S(1)}, u32[]{:S(2)}) copy-start(s32[1024]{0:T(1024)S(1)} %pad_clamp_fusion.1) | copy-start | bytes 12292
  22.1 23.8 %copy-start.57 = (pred[4,128]{1,0:T(4,128)(4,1)}, pred[4,128]{1,0:T(4,128)(4,1)S(1)}, u32[]{:S(2)}) copy-start(pred[4,128]{1,0:T(4,128)(4,1)S(1)} %get-tuple-element.224) | copy-start | bytes 1540
  22.1 44.1 %copy-start.60 = (pred[4,128]{1,0:T(4,128)(4,1)}, pred[4,128]{1,0:T(4,128)(4,1)S(1)}, u32[]{:S(2)}) copy-start(pred[4,128]{1,0:T(4,128)(4,1)S(1)} %get-tuple-element.223) | copy-start | bytes 1540
  22.1 12.3 %all-to-all-start.4 = ((bf16[4,2,8192]{2,1,0:T(2,128)(2,1)}), bf16[4,2,8192]{2,1,0:T(2,128)(2,1)S(1)}, u32[]{:S(2)}, u32[]{:S(2)}) async-start(bf16[4,2,8192]{2,1,0:T(2,128)(2,1)} %reshape.901), calls=%async_computation.4 | async-start | bytes 262144 | tf_op jit(solution)/shard_map/all_to_all | solution.py:58
  34.4 8.0 %all-to-all-start.1 = ((bf16[4,2,8192]{2,1,0:T(2,128)(2,1)}), bf16[4,2,8192]{2,1,0:T(2,128)(2,1)S(1)}, u32[]{:S(2)}, u32[]{:S(2)}) async-start(bf16[4,2,8192]{2,1,0:T(2,128)(2,1)} %reshape.895), calls=%async_computation.1 | async-start | bytes 262144 | tf_op jit(solution)/shard_map/all_to_all | solution.py:71
  37.7 24.5 %copy-start.54 = (pred[4]{0:T(512)(128)(4,1)}, pred[4]{0:T(512)(128)(4,1)S(1)}, u32[]{:S(2)}) copy-start(pred[4]{0:T(512)(128)(4,1)S(1)} %compare_and_fusion.1) | copy-start | bytes 16
  53.5 7.9 %all-to-all-start.2 = ((bf16[4,2,8192]{2,1,0:T(2,128)(2,1)}), bf16[4,2,8192]{2,1,0:T(2,128)(2,1)S(1)}, u32[]{:S(2)}, u32[]{:S(2)}) async-start(bf16[4,2,8192]{2,1,0:T(2,128)(2,1)} %reshape.897), calls=%async_computation.2 | async-start | bytes 262144 | tf_op jit(solution)/shard_map/all_to_all | solution.py:71
  91.1 8.1 %all-to-all-start.5 = ((bf16[4,2,8192]{2,1,0:T(2,128)(2,1)}), bf16[4,2,8192]{2,1,0:T(2,128)(2,1)S(1)}, u32[]{:S(2)}, u32[]{:S(2)}) async-start(bf16[4,2,8192]{2,1,0:T(2,128)(2,1)} %reshape.903), calls=%async_computation.5 | async-start | bytes 262144 | tf_op jit(solution)/shard_map/all_to_all | solution.py:81
  99.2 15.9 %all-to-all-start.3 = ((bf16[4,2,8192]{2,1,0:T(2,128)(2,1)}), bf16[4,2,8192]{2,1,0:T(2,128)(2,1)}, u32[]{:S(2)}, u32[]{:S(2)}) async-start(bf16[4,2,8192]{2,1,0:T(2,128)(2,1)} %reshape.899), calls=%async_computation.3 | async-start | bytes 262144 | tf_op jit(solution)/shard_map/all_to_all | solution.py:64
  126.2 8.1 %all-to-all-start.6 = ((bf16[4,2,8192]{2,1,0:T(2,128)(2,1)}), bf16[4,2,8192]{2,1,0:T(2,128)(2,1)S(1)}, u32[]{:S(2)}, u32[]{:S(2)}) async-start(bf16[4,2,8192]{2,1,0:T(2,128)(2,1)} %reshape.905), calls=%async_computation.6 | async-start | bytes 262144 | tf_op jit(solution)/shard_map/all_to_all | solution.py:81
  129.7 137.5 %all-reduce.87.cloned.1.call-start = ((), (), s32[]{:S(2)}) async-start(), calls=%async_computation.8 | async-start | bytes 393216 | tf_op jit(solution)/shard_map/psum | solution.py:191
  193.8 8.2 %all-to-all-start.7 = ((bf16[4,2,8192]{2,1,0:T(2,128)(2,1)}), bf16[4,2,8192]{2,1,0:T(2,128)(2,1)S(1)}, u32[]{:S(2)}, u32[]{:S(2)}) async-start(bf16[4,2,8192]{2,1,0:T(2,128)(2,1)} %reshape.907), calls=%async_computation.7 | async-start | bytes 262144 | tf_op jit(solution)/shard_map/all_to_all | solution.py:64
  (129 other events, 297.4 us)
Sparse Core Ops, SparseCore 0:
  143.2 123.9 all-reduce.86
where the time goes:
time: 278 us; the launch traced here: 276 us
  waiting for transfers between devices  79.8 us (29%)
  local copies, waits for them, and re-layouts  62.6 us (23%)
  blocking collectives  40.5 us (15%)
  other arithmetic  38.4 us (14%)
  starting transfers between devices  29.1 us (10%)
  between operations  16.4 us (6%)
  matrix products  8.95 us (3%)
    psum x1, waiting for transfers between devices, body(): lax.psum((mix_stack, kernel_stack, gain_stack), ('line', 'dp'))  64.4 us
    psum x1, blocking collectives, body(): lax.psum((mix_stack, kernel_stack, gain_stack), ('line', 'dp'))  40.5 us
    unnamed x314, local copies, waits for them, and re-layouts  26.4 us
    unnamed x8, other arithmetic  12.3 us
    slice x21, local copies, waits for them, and re-layouts, shifted(): values[:, offset:]  12 us
    all_to_all x2, starting transfers between devices, into_lines(): lax.all_to_all(rolled, 'line', split_axis=1, concat_axis=1, tiled=True)  7.74 us
    all_to_all x2, starting transfers between devices, out_of_lines(): lax.all_to_all(placed, 'line', split_axis=1, concat_axis=1, tiled=True)  7.7 us
    scatter x5, local copies, waits for them, and re-layouts, unpermute(): return jnp.zeros_like(array).at[:, table].set(array)  7.64 us
  transfers between devices with their start and end apart: 9, of which 6 were waited for; matrix products, arithmetic and copies ran while one was open for 13% of the time, Pallas kernels for 0%

commit v1 on v0

v1 whole, which is shorter than its diff:
```python
import functools

import jax
import jax.numpy as jnp
from jax import lax
from jax.experimental import pallas as pl
from jax.experimental.pallas import tpu as pltpu
from jax.sharding import PartitionSpec as P

EPSILON = 1e-06
EDGE = 8
F32 = jnp.float32
BF16 = jnp.bfloat16


def tap_offsets(taps):
    offsets = [0]
    for dilation_level in range((taps - 1) // 2):
        offsets = offsets + [-(2**dilation_level), 2**dilation_level]
    return offsets


def fold(values):
    return jnp.sum(values.reshape(-1, 8, values.shape[1]), axis=0)


def kernel_body(
    shape,
    fields,
    cotangent,
    gain_ref,
    taps_ref,
    mix_ref,
    order_ref,
    starts_ref,
    imitated,
    field_grad,
    mix_out,
    taps_out,
    gain_out,
    gather,
    scatter,
    recv,
    placed,
    stream,
    scaled,
    inverse,
    masked,
    slope,
    activated,
    grads,
    padded,
    sums,
    parts,
    a_recv,
    b_recv,
    full,
    ex_send,
    ex_recv,
    a_send,
    a_arrive,
    b_send,
    b_arrive,
    c_send,
    c_arrive,
    local_sem,
):
    ranks, copies, line_len, scale = shape
    cells, channels = stream.shape
    lines = cells // line_len
    block = cells // ranks
    taps = taps_ref.shape[1]
    offsets = tap_offsets(taps)
    piece = parts.shape[1] // ranks
    me = lax.axis_index("line")
    my_dp = lax.axis_index("dp")

    def peer(step):
        return lax.rem(me + step, ranks)

    def dp_peer(step):
        return lax.rem(my_dp + step, copies)

    def rows(index, size):
        return pl.ds(pl.multiple_of(index * size, size), size)

    barrier = pltpu.get_barrier_semaphore()
    for step in range(1, ranks):
        pl.semaphore_signal(
            barrier, inc=1, device_id={"line": peer(step)}, device_id_type=pl.DeviceIdType.MESH
        )
    for step in range(1, copies):
        pl.semaphore_signal(
            barrier, inc=1, device_id={"dp": dp_peer(step)}, device_id_type=pl.DeviceIdType.MESH
        )
    pl.semaphore_wait(barrier, ranks - 1 + copies - 1)

    unsent = []

    def send(stage, step, source, target):
        copy = pltpu.make_async_remote_copy(
            src_ref=source,
            dst_ref=target,
            send_sem=ex_send.at[stage, step],
            recv_sem=ex_recv.at[stage, step],
            device_id={"line": peer(step)},
            device_id_type=pl.DeviceIdType.MESH,
        )
        copy.start()
        unsent.append(copy)
        return copy

    def enter(stage, array, shift):
        out = []
        for step in range(1, ranks):
            chunk = lax.rem(peer(step) + ranks * shift - shift * me, ranks)
            out.append(
                send(stage, step, array.at[0, rows(chunk, block)], recv.at[stage, rows(me, block)])
            )
        chunk = lax.rem(me + ranks * shift - shift * me, ranks)
        own = pltpu.make_async_copy(
            array.at[0, rows(chunk, block)], recv.at[stage, rows(me, block)], local_sem.at[stage]
        )
        own.start()
        return out, own

    arriving, own_fields = enter(0, fields, 0)

    def tables(direction):
        row = order_ref[direction : direction + 1, :]
        lanes = 128
        across = lax.broadcasted_iota(jnp.int32, (cells, cells), 0)
        scatter[direction] = jnp.where(across == row, 1.0, 0.0).astype(BF16)
        turned = jnp.transpose(jnp.broadcast_to(row, (lanes, cells)))
        for first in range(0, cells, lanes):
            width = lax.broadcasted_iota(jnp.int32, (cells, lanes), 1) + first
            gather[direction, :, first : first + lanes] = jnp.where(
                turned == width, 1.0, 0.0
            ).astype(BF16)

    tables(0)
    padded[...] = jnp.zeros_like(padded)
    parts[...] = jnp.zeros_like(parts)

    def hand_over(stage, direction, values, sign):
        out = []
        for anchor in list(range(1, ranks)) + [0]:
            span = pl.ds(anchor * block, block)
            chunk = jnp.dot(
                scatter[direction, span, :], values, preferred_element_type=F32
            ).astype(BF16)
            if anchor:
                placed[stage, span, :] = chunk
                step = (sign * anchor) % ranks
                out.append(send(stage, step, placed.at[stage, span], recv.at[stage, span]))
            else:
                recv[stage, span, :] = chunk
        return out

    def leave(stage, direction, values, target):
        chunk = jnp.dot(scatter[direction], values, preferred_element_type=F32)
        placed[stage] = chunk.astype(BF16)
        out = []
        for step in range(1, ranks):
            anchor = peer(step)
            where = lax.rem(me + direction * (ranks - anchor), ranks)
            out.append(
                send(
                    stage, step, placed.at[stage, rows(anchor, block)],
                    target.at[0, rows(where, block)],
                )
            )
        where = lax.rem(me + direction * (ranks - me), ranks)
        own = pltpu.make_async_copy(
            placed.at[stage, rows(me, block)], target.at[0, rows(where, block)],
            local_sem.at[stage],
        )
        own.start()
        return out, own

    def take(stage, direction, copies_in):
        for copy in copies_in:
            copy.wait_recv()
        return jnp.dot(gather[direction], recv[stage], preferred_element_type=F32)

    def keep_rows(direction, line):
        position = lax.broadcasted_iota(jnp.int32, (line_len, channels), 0)
        return position >= starts_ref[direction, line]

    def forward(direction):
        def one_line(line, carry):
            here = rows(line, line_len)
            values = stream[here, :]
            norm = lax.rsqrt(jnp.mean(values * values, axis=-1, keepdims=True) + EPSILON)
            ratio = values * norm
            normed = (ratio * gain_ref[direction : direction + 1, :]).astype(BF16).astype(F32)
            inputs = jnp.where(keep_rows(direction, line), normed, 0.0)
            padded[pl.ds(EDGE, line_len), :] = inputs
            inverse[direction, here, :] = jnp.broadcast_to(norm, (line_len, channels))
            scaled[direction, here, :] = ratio
            masked[direction, here, :] = inputs
            hidden = taps_ref[direction, 0:1, :] * inputs
            for tap in range(1, taps):
                offset = offsets[tap]
                weight = taps_ref[direction, tap : tap + 1, :]
                size = abs(offset)
                if size < EDGE:
                    hidden = hidden + weight * padded[pl.ds(EDGE + offset, line_len), :]
                elif offset > 0:
                    inner = hidden[: line_len - size] + weight * inputs[size:]
                    hidden = jnp.concatenate([inner, hidden[line_len - size :]], axis=0)
                else:
                    inner = hidden[size:] + weight * inputs[: line_len - size]
                    hidden = jnp.concatenate([hidden[:size], inner], axis=0)
            gate = 0.5 * jnp.tanh(0.5 * hidden) + 0.5
            activated[direction, here, :] = (hidden * gate).astype(BF16)
            slope[direction, here, :] = gate * (1.0 + hidden * (1.0 - gate))
            return carry

        lax.fori_loop(0, lines, one_line, 0)
        mixed = jnp.dot(activated[direction], mix_ref[direction], preferred_element_type=F32)
        return (stream[...] + mixed.astype(BF16).astype(F32)).astype(BF16)

    own_fields.wait()
    stream[...] = take(0, 0, arriving)
    cot_arriving, own_cot = enter(1, cotangent, 2)
    moved = forward(0)
    arriving = hand_over(2, 0, moved, 1)
    tables(1)
    stream[...] = take(2, 1, arriving)
    moved = forward(1)
    arriving = hand_over(3, 1, moved, 1)
    tables(2)
    stream[...] = take(3, 2, arriving)
    moved = forward(2)
    out_arriving, own_out = leave(4, 2, moved, imitated)
    own_cot.wait()
    grads[...] = take(1, 2, cot_arriving)

    def backward(direction):
        grad_mixed = grads[...].astype(BF16)
        parts[direction, :channels, :] = lax.dot_general(
            activated[direction], grad_mixed, (((0,), (0,)), ((), ())), preferred_element_type=F32
        )
        stream[...] = lax.dot_general(
            grad_mixed, mix_ref[direction], (((1,), (1,)), ((), ())), preferred_element_type=F32
        )
        sums[...] = jnp.zeros_like(sums)

        def one_line(line, carry):
            here = rows(line, line_len)
            grad = (stream[here, :] * slope[direction, here, :]).astype(BF16).astype(F32)
            padded[pl.ds(EDGE, line_len), :] = grad
            inputs = masked[direction, here, :]
            total = taps_ref[direction, 0:1, :] * grad
            sums[0:8, :] += fold(grad * inputs)
            for tap in range(1, taps):
                offset = -offsets[tap]
                weight = taps_ref[direction, tap : tap + 1, :]
                size = abs(offset)
                slot = pl.ds(8 * tap, 8)
                if size < EDGE:
                    near = padded[pl.ds(EDGE + offset, line_len), :]
                    total = total + weight * near
                    sums[slot, :] += fold(near * inputs)
                elif offset > 0:
                    near = grad[size:]
                    inner = total[: line_len - size] + weight * near
                    total = jnp.concatenate([inner, total[line_len - size :]], axis=0)
                    sums[slot, :] += fold(near * inputs[: line_len - size])
                else:
                    near = grad[: line_len - size]
                    inner = total[size:] + weight * near
                    total = jnp.concatenate([total[:size], inner], axis=0)
                    sums[slot, :] += fold(near * inputs[size:])
            cell = jnp.where(keep_rows(direction, line), total, 0.0).astype(BF16).astype(F32)
            ratio = scaled[direction, here, :]
            sums[8 * taps : 8 * taps + 8, :] += fold(cell * ratio)
            weighted = cell * gain_ref[direction : direction + 1, :]
            centre = jnp.mean(weighted * ratio, axis=-1, keepdims=True)
            change = inverse[direction, here, :] * (weighted - ratio * centre)
            grads[here, :] = grads[here, :] + change
            return carry

        lax.fori_loop(0, lines, one_line, 0)
        parts[direction, channels : channels + taps + 1, :] = jnp.sum(
            sums[...].reshape(taps + 1, 8, channels), axis=1
        )
        return grads[...].astype(BF16)

    def reduce_line(direction):
        out = []
        for step in range(1, ranks):
            copy = pltpu.make_async_remote_copy(
                src_ref=parts.at[direction, rows(peer(step), piece)],
                dst_ref=a_recv.at[direction, step],
                send_sem=a_send.at[direction, step],
                recv_sem=a_arrive.at[direction, step],
                device_id={"line": peer(step)},
                device_id_type=pl.DeviceIdType.MESH,
            )
            copy.start()
            unsent.append(copy)
            out.append(copy)
        return out

    def reduce_dp(direction, copies_in):
        total = parts[direction, rows(me, piece), :]
        for step in range(1, ranks):
            copies_in[step - 1].wait_recv()
            total = total + a_recv[direction, step]
        b_recv[direction, my_dp] = total
        out = []
        for step in range(1, copies):
            copy = pltpu.make_async_remote_copy(
                src_ref=b_recv.at[direction, my_dp],
                dst_ref=b_recv.at[direction, my_dp],
                send_sem=b_send.at[direction, step],
                recv_sem=b_arrive.at[direction, step],
                device_id={"dp": dp_peer(step)},
                device_id_type=pl.DeviceIdType.MESH,
            )
            copy.start()
            unsent.append(copy)
            out.append(copy)
        return out

    def spread(direction, copies_in):
        for copy in copies_in:
            copy.wait_recv()
        total = b_recv[direction, 0]
        for index in range(1, copies):
            total = total + b_recv[direction, index]
        full[direction, rows(me, piece), :] = total * scale
        out = []
        for step in range(1, ranks):
            copy = pltpu.make_async_remote_copy(
                src_ref=full.at[direction, rows(me, piece)],
                dst_ref=full.at[direction, rows(me, piece)],
                send_sem=c_send.at[direction, step],
                recv_sem=c_arrive.at[direction, step],
                device_id={"line": peer(step)},
                device_id_type=pl.DeviceIdType.MESH,
            )
            copy.start()
            unsent.append(copy)
            out.append(copy)
        return out

    def finish(direction, copies_in):
        for copy in copies_in:
            copy.wait_recv()
        mix_out[direction] = full[direction, :channels, :]
        taps_out[direction] = full[direction, channels : channels + taps, :]
        gain_out[direction : direction + 1, :] = full[
            direction, channels + taps : channels + taps + 1, :
        ]

    moved = backward(2)
    arriving = hand_over(5, 2, moved, -1)
    a2 = reduce_line(2)
    grads[...] = take(5, 1, arriving)
    moved = backward(1)
    arriving = hand_over(6, 1, moved, -1)
    a1 = reduce_line(1)
    b2 = reduce_dp(2, a2)
    grads[...] = take(6, 0, arriving)
    moved = backward(0)
    a0 = reduce_line(0)
    last_arriving, own_last = leave(7, 0, moved, field_grad)
    b1 = reduce_dp(1, a1)
    c2 = spread(2, b2)
    b0 = reduce_dp(0, a0)
    c1 = spread(1, b1)
    finish(2, c2)
    c0 = spread(0, b0)
    finish(1, c1)
    finish(0, c0)
    for copy in out_arriving + last_arriving:
        copy.wait_recv()
    own_out.wait()
    own_last.wait()
    for copy in unsent:
        copy.wait_send()


def body(fields, cotangent, norm_gain, kernel, mix_weight, line_order, line_starts):
    ranks = lax.axis_size("line")
    copies = lax.axis_size("dp")
    batch, cells, channels = fields.shape
    assert batch == 1
    directions, taps = kernel.shape[:2]
    line_len = cells // line_starts.shape[1]
    scale = float(copies * batch * ranks * cells) ** (-0.5)
    unit = 8 * ranks
    part_rows = -(-(channels + taps + 1) // unit) * unit
    piece = part_rows // ranks
    stages = 2 * directions + 2
    vmem = pl.BlockSpec(memory_space=pltpu.VMEM)
    smem = pl.BlockSpec(memory_space=pltpu.SMEM)
    anywhere = pl.BlockSpec(memory_space=pl.ANY)
    wide = pltpu.VMEM((directions, cells, channels), F32)
    dma = pltpu.SemaphoreType.DMA
    return pl.pallas_call(
        functools.partial(kernel_body, (ranks, copies, line_len, scale)),
        out_shape=(
            jax.ShapeDtypeStruct(fields.shape, BF16),
            jax.ShapeDtypeStruct(fields.shape, BF16),
            jax.ShapeDtypeStruct((directions, channels, channels), F32),
            jax.ShapeDtypeStruct((directions, taps, channels), F32),
            jax.ShapeDtypeStruct((directions, channels), F32),
        ),
        in_specs=[anywhere, anywhere, vmem, vmem, vmem, vmem, smem],
        out_specs=(anywhere, anywhere, vmem, vmem, vmem),
        scratch_shapes=[
            pltpu.VMEM((directions, cells, cells), BF16),
            pltpu.VMEM((directions, cells, cells), BF16),
            pltpu.VMEM((stages, cells, channels), BF16),
            pltpu.VMEM((stages, cells, channels), BF16),
            pltpu.VMEM((cells, channels), F32),
            wide,
            wide,
            wide,
            wide,
            pltpu.VMEM((directions, cells, channels), BF16),
            pltpu.VMEM((cells, channels), F32),
            pltpu.VMEM((line_len + 2 * EDGE, channels), F32),
            pltpu.VMEM(((taps + 1) * 8, channels), F32),
            pltpu.VMEM((directions, part_rows, channels), F32),
            pltpu.VMEM((directions, ranks, piece, channels), F32),
            pltpu.VMEM((directions, copies, piece, channels), F32),
            pltpu.VMEM((directions, part_rows, channels), F32),
            dma((stages, ranks)),
            dma((stages, ranks)),
            dma((directions, ranks)),
            dma((directions, ranks)),
            dma((directions, copies)),
            dma((directions, copies)),
            dma((directions, ranks)),
            dma((directions, ranks)),
            dma((stages,)),
        ],
        compiler_params=pltpu.CompilerParams(
            collective_id=0, has_side_effects=True, vmem_limit_bytes=40 * 1024 * 1024
        ),
        name="mesh_block",
    )(fields, cotangent, norm_gain, kernel, mix_weight, line_order, line_starts)


def solution(mesh):
    in_specs = (
        P("dp", "line", None),
        P("dp", "line", None),
        P(),
        P(),
        P(),
        P(None, "line"),
        P(None, "line"),
    )
    out_specs = (P("dp", "line", None), P("dp", "line", None), P(), P(), P())
    return jax.shard_map(body, mesh=mesh, in_specs=in_specs, out_specs=out_specs, check_vma=False)
```

time: 278 us -> 55 us (0.20)
  waiting for transfers between devices: 79.8 us -> 0 us
  local copies, waits for them, and re-layouts: 62.6 us -> 8.66 us
  Pallas kernels: 0 us -> 45.3 us
  blocking collectives: 40.5 us -> 0 us
  other arithmetic: 38.4 us -> 0 us
  starting transfers between devices: 29.1 us -> 0 us
  between operations: 16.4 us -> 0.66 us
  matrix products: 8.95 us -> 0 us
    psum x1 -> x0, waiting for transfers between devices: 64.4 us -> none  [body(): lax.psum((mix_stack, kernel_stack, gain_stack), ('line', 'dp'))]
    pallas_call x0 -> x1, Pallas kernels: none -> 45.3 us  [body(): pl.pallas_call(functools.partial(kernel_body, (ranks, copies, line_len, s...]
    psum x1 -> x0, blocking collectives: 40.5 us -> none  [body(): lax.psum((mix_stack, kernel_stack, gain_stack), ('line', 'dp'))]
    all_to_all x8 -> x0, starting transfers between devices: 29 us -> none  [the longest x2 7.74 us: into_lines(): lax.all_to_all(rolled, 'line', split_axis=1, concat_axis=1, tiled=True)]
    unnamed x314 -> x19, local copies, waits for them, and re-layouts: 26.4 us -> 8.66 us
    all_to_all x8 -> x0, waiting for transfers between devices: 15.4 us -> none  [the longest x2 7.54 us: advance(): lax.all_to_all(rolled, 'line', split_axis=1, concat_axis=1, tiled=True)]
    slice x43 -> x0, local copies, waits for them, and re-layouts: 12.7 us -> none  [the longest x21 12 us: shifted(): values[:, offset:]]
    unnamed x8 -> x0, other arithmetic: 12.3 us -> none
  transfers between devices with their start and end apart: 9 -> 0, of which waited for: 6 -> 0; matrix products, arithmetic and copies ran while one was open for 13% -> 0% of each run, Pallas kernels for 0% -> 0%
where the time goes in v1:
time: 55 us; the launch traced here: 54.6 us
  Pallas kernels  45.3 us (82%)
  local copies, waits for them, and re-layouts  8.66 us (16%)
  between operations  0.66 us (1%)
    pallas_call x1, Pallas kernels, body(): pl.pallas_call(functools.partial(kernel_body, (ranks, copies, line_len, s...  45.3 us
    unnamed x19, local copies, waits for them, and re-layouts  8.66 us

profile of v1, /device:TPU:0, one launch (start us, length us, event | category | flops | bytes accessed | tf_op | source)
XLA Modules:
  0.0 54.6 jit_solution(16416903358945417392)
XLA Ops:
  0.6 0.0 copy-start
  0.6 0.9 %copy-done = bf16[1,512,128]{2,1,0:T(8,128)(2,1)S(1)} copy-done((bf16[1,512,128]{2,1,0:T(8,128)(2,1)S(1)}, bf16[1,512,128]{2,1,0:T(8,128)(2,1)}, u32[]{:S(2)}) %copy-start) | copy-done | bytes 131096
  1.5 0.0 copy-start.1
  1.5 0.9 %copy-done.1 = bf16[1,512,128]{2,1,0:T(8,128)(2,1)S(1)} copy-done((bf16[1,512,128]{2,1,0:T(8,128)(2,1)S(1)}, bf16[1,512,128]{2,1,0:T(8,128)(2,1)}, u32[]{:S(2)}) %copy-start.1) | copy-done | bytes 131096
  2.4 0.0 copy-start.2
  2.4 0.9 %copy-done.2 = bf16[3,128,128]{2,1,0:T(8,128)(2,1)S(1)} copy-done((bf16[3,128,128]{2,1,0:T(8,128)(2,1)S(1)}, bf16[3,128,128]{2,1,0:T(8,128)(2,1)}, u32[]{:S(2)}) %copy-start.2) | copy-done | bytes 98328
  3.3 0.0 copy-start.3
  3.3 0.7 %copy-done.3 = f32[3,15,128]{2,1,0:T(8,128)S(1)} copy-done((f32[3,15,128]{2,1,0:T(8,128)S(1)}, f32[3,15,128]{2,1,0:T(8,128)}, u32[]{:S(2)}) %copy-start.3) | copy-done | bytes 23064
  4.1 0.0 copy-start.4
  4.1 0.7 %copy-done.4 = s32[3,512]{1,0:T(4,128)S(1)} copy-done((s32[3,512]{1,0:T(4,128)S(1)}, s32[3,512]{1,0:T(4,128)}, u32[]{:S(2)}) %copy-start.4) | copy-done | bytes 6168
  4.8 0.0 copy-start.5
  4.8 0.7 %copy-done.5 = f32[3,128]{1,0:T(4,128)S(1)} copy-done((f32[3,128]{1,0:T(4,128)S(1)}, f32[3,128]{1,0:T(4,128)}, u32[]{:S(2)}) %copy-start.5) | copy-done | bytes 1560
  5.5 0.0 copy-start.6
  5.5 0.7 %copy-done.6 = s32[3,4]{1,0:T(4,128)S(1)} copy-done((s32[3,4]{1,0:T(4,128)S(1)}, s32[3,4]{1,0:T(4,128)}, u32[]{:S(2)}) %copy-start.6) | copy-done | bytes 72
  6.1 45.3 %mesh_block.1 = (bf16[1,512,128]{2,1,0:T(8,128)(2,1)S(1)}, bf16[1,512,128]{2,1,0:T(8,128)(2,1)S(1)}, f32[3,128,128]{2,1,0:T(8,128)S(1)}, f32[3,15,128]{2,1,0:T(8,128)S(1)}, f32[3,128]{1,0:T(4,128)S(1)}) custom-call(bf16[1,512,128]{2,1,0:T(8,128)(2,1)S(1)} %copy-done, bf16[1,512,128]{2,1,0:T(8,128)(2,1)S(1)} %copy-done.1, f32[3,128]{1,0:T(4,128)S(1)} %copy-done.5, ...), custom_call_target="tpu_custom_call" | custom-call | tf_op jit(solution)/shard_map/mesh_block/pallas_call | solution.py:404
  51.5 0.7 %copy.17 = bf16[1,512,128]{2,1,0:T(8,128)(2,1)} copy(bf16[1,512,128]{2,1,0:T(8,128)(2,1)S(1)} %get-tuple-element.10) | data formatting | bytes 262144
  52.1 0.7 %copy.18 = bf16[1,512,128]{2,1,0:T(8,128)(2,1)} copy(bf16[1,512,128]{2,1,0:T(8,128)(2,1)S(1)} %get-tuple-element.11) | data formatting | bytes 262144
  52.8 0.7 %copy.19 = f32[3,128,128]{2,1,0:T(8,128)} copy(f32[3,128,128]{2,1,0:T(8,128)S(1)} %get-tuple-element.12) | data formatting | bytes 393216
  53.4 0.6 %copy.20 = f32[3,15,128]{2,1,0:T(8,128)} copy(f32[3,15,128]{2,1,0:T(8,128)S(1)} %get-tuple-element.13) | data formatting | bytes 46080
  54.1 0.6 %copy.21 = f32[3,128]{1,0:T(4,128)} copy(f32[3,128]{1,0:T(4,128)S(1)} %get-tuple-element.14) | data formatting | bytes 3072
Async XLA Ops:
  0.6 0.9 %copy-start = (bf16[1,512,128]{2,1,0:T(8,128)(2,1)S(1)}, bf16[1,512,128]{2,1,0:T(8,128)(2,1)}, u32[]{:S(2)}) copy-start(bf16[1,512,128]{2,1,0:T(8,128)(2,1)} %fields.1) | copy-start | bytes 393220
  1.5 0.9 %copy-start.1 = (bf16[1,512,128]{2,1,0:T(8,128)(2,1)S(1)}, bf16[1,512,128]{2,1,0:T(8,128)(2,1)}, u32[]{:S(2)}) copy-start(bf16[1,512,128]{2,1,0:T(8,128)(2,1)} %cotangent.1) | copy-start | bytes 393220
  2.4 0.9 %copy-start.2 = (bf16[3,128,128]{2,1,0:T(8,128)(2,1)S(1)}, bf16[3,128,128]{2,1,0:T(8,128)(2,1)}, u32[]{:S(2)}) copy-start(bf16[3,128,128]{2,1,0:T(8,128)(2,1)} %mix_ref.1) | copy-start | bytes 294916
  3.3 0.7 %copy-start.3 = (f32[3,15,128]{2,1,0:T(8,128)S(1)}, f32[3,15,128]{2,1,0:T(8,128)}, u32[]{:S(2)}) copy-start(f32[3,15,128]{2,1,0:T(8,128)} %taps_ref.1) | copy-start | bytes 69124
  4.1 0.7 %copy-start.4 = (s32[3,512]{1,0:T(4,128)S(1)}, s32[3,512]{1,0:T(4,128)}, u32[]{:S(2)}) copy-start(s32[3,512]{1,0:T(4,128)} %order_ref.1) | copy-start | bytes 18436
  4.8 0.7 %copy-start.5 = (f32[3,128]{1,0:T(4,128)S(1)}, f32[3,128]{1,0:T(4,128)}, u32[]{:S(2)}) copy-start(f32[3,128]{1,0:T(4,128)} %gain_ref.1) | copy-start | bytes 4612
  5.5 0.7 %copy-start.6 = (s32[3,4]{1,0:T(4,128)S(1)}, s32[3,4]{1,0:T(4,128)}, u32[]{:S(2)}) copy-start(s32[3,4]{1,0:T(4,128)} %starts_ref.1) | copy-start | bytes 148

commit v2 on v1

v2 whole, which is shorter than its diff:
```python
import functools

import jax
import jax.numpy as jnp
from jax import lax
from jax.experimental import pallas as pl
from jax.experimental.pallas import tpu as pltpu
from jax.sharding import PartitionSpec as P

EPSILON = 1e-06
EDGE = 8
F32 = jnp.float32
BF16 = jnp.bfloat16


def tap_offsets(taps):
    offsets = [0]
    for dilation_level in range((taps - 1) // 2):
        offsets = offsets + [-(2**dilation_level), 2**dilation_level]
    return offsets


def fold(values):
    return jnp.sum(values.reshape(-1, 8, values.shape[1]), axis=0)


def kernel_body(
    shape,
    fields,
    cotangent,
    gain_hbm,
    taps_hbm,
    mix_hbm,
    order_hbm,
    starts_hbm,
    imitated,
    field_grad,
    mix_out,
    taps_out,
    gain_out,
    gain_ref,
    taps_ref,
    mix_ref,
    order_ref,
    starts_ref,
    gather,
    scatter,
    recv,
    placed,
    stream,
    scaled,
    inverse,
    masked,
    slope,
    activated,
    grads,
    padded,
    sums,
    parts,
    a_recv,
    b_recv,
    full,
    line_tails,
    dp_tails,
    ex_send,
    ex_recv,
    a_send,
    a_arrive,
    b_send,
    b_arrive,
    c_send,
    c_arrive,
    t_send,
    t_arrive,
    u_send,
    u_arrive,
    local_sem,
    load_sem,
):
    ranks, copies, line_len, scale = shape
    cells, channels = stream.shape
    lines = cells // line_len
    block = cells // ranks
    taps = taps_ref.shape[1]
    offsets = tap_offsets(taps)
    piece = parts.shape[1] // ranks
    me = lax.axis_index("line")
    my_dp = lax.axis_index("dp")

    loads = []
    for index, (source, target) in enumerate(
        (
            (order_hbm, order_ref),
            (gain_hbm, gain_ref),
            (taps_hbm, taps_ref),
            (starts_hbm, starts_ref),
            (mix_hbm, mix_ref),
        )
    ):
        load = pltpu.make_async_copy(source, target, load_sem.at[index])
        load.start()
        loads.append(load)

    def peer(step):
        return lax.rem(me + step, ranks)

    def dp_peer(step):
        return lax.rem(my_dp + step, copies)

    def rows(index, size):
        return pl.ds(pl.multiple_of(index * size, size), size)

    barrier = pltpu.get_barrier_semaphore()
    for step in range(1, ranks):
        pl.semaphore_signal(
            barrier, inc=1, device_id={"line": peer(step)}, device_id_type=pl.DeviceIdType.MESH
        )
    for step in range(1, copies):
        pl.semaphore_signal(
            barrier, inc=1, device_id={"dp": dp_peer(step)}, device_id_type=pl.DeviceIdType.MESH
        )
    pl.semaphore_wait(barrier, ranks - 1 + copies - 1)

    unsent = []

    def remote(source, target, send_sem, recv_sem, where):
        copy = pltpu.make_async_remote_copy(
            src_ref=source,
            dst_ref=target,
            send_sem=send_sem,
            recv_sem=recv_sem,
            device_id=where,
            device_id_type=pl.DeviceIdType.MESH,
        )
        copy.start()
        unsent.append(copy)
        return copy

    def send(stage, step, source, target):
        return remote(
            source, target, ex_send.at[stage, step], ex_recv.at[stage, step], {"line": peer(step)}
        )

    def enter(stage, array, shift):
        out = []
        for step in range(1, ranks):
            chunk = lax.rem(peer(step) + ranks * shift - shift * me, ranks)
            out.append(
                send(stage, step, array.at[0, rows(chunk, block)], recv.at[stage, rows(me, block)])
            )
        chunk = lax.rem(me + ranks * shift - shift * me, ranks)
        own = pltpu.make_async_copy(
            array.at[0, rows(chunk, block)], recv.at[stage, rows(me, block)], local_sem.at[stage]
        )
        own.start()
        return out, own

    arriving, own_fields = enter(0, fields, 0)

    def tables(direction):
        row = order_ref[direction : direction + 1, :]
        lanes = 128
        across = lax.broadcasted_iota(jnp.int32, (cells, cells), 0)
        scatter[direction] = jnp.where(across == row, 1.0, 0.0).astype(BF16)
        turned = jnp.transpose(jnp.broadcast_to(row, (lanes, cells)))
        for first in range(0, cells, lanes):
            width = lax.broadcasted_iota(jnp.int32, (cells, lanes), 1) + first
            gather[direction, :, first : first + lanes] = jnp.where(
                turned == width, 1.0, 0.0
            ).astype(BF16)

    masked[...] = jnp.zeros_like(masked)
    padded[...] = jnp.zeros_like(padded)
    for load in loads:
        load.wait()
    tables(0)

    def hand_over(stage, direction, values, sign):
        out = []
        for anchor in list(range(1, ranks)) + [0]:
            span = pl.ds(anchor * block, block)
            chunk = jnp.dot(
                scatter[direction, span, :], values, preferred_element_type=F32
            ).astype(BF16)
            if anchor:
                placed[stage, span, :] = chunk
                step = (sign * anchor) % ranks
                out.append(send(stage, step, placed.at[stage, span], recv.at[stage, span]))
            else:
                recv[stage, span, :] = chunk
        return out

    def leave(stage, direction, values, target):
        chunk = jnp.dot(scatter[direction], values, preferred_element_type=F32)
        placed[stage] = chunk.astype(BF16)
        out = []
        for step in range(1, ranks):
            anchor = peer(step)
            where = lax.rem(me + direction * (ranks - anchor), ranks)
            out.append(
                send(
                    stage,
                    step,
                    placed.at[stage, rows(anchor, block)],
                    target.at[0, rows(where, block)],
                )
            )
        where = lax.rem(me + direction * (ranks - me), ranks)
        own = pltpu.make_async_copy(
            placed.at[stage, rows(me, block)],
            target.at[0, rows(where, block)],
            local_sem.at[stage],
        )
        own.start()
        return out, own

    def take(stage, direction, copies_in):
        for copy in copies_in:
            copy.wait_recv()
        return jnp.dot(gather[direction], recv[stage], preferred_element_type=F32)

    def keep_rows(direction, line):
        position = lax.broadcasted_iota(jnp.int32, (line_len, channels), 0)
        return position >= starts_ref[direction : direction + 1, line : line + 1]

    inside = pl.ds(EDGE, line_len)

    def forward(direction):
        for line in range(lines):
            here = pl.ds(line * line_len, line_len)
            values = stream[here, :]
            norm = lax.rsqrt(jnp.mean(values * values, axis=-1, keepdims=True) + EPSILON)
            ratio = values * norm
            normed = (ratio * gain_ref[direction : direction + 1, :]).astype(BF16).astype(F32)
            masked[direction, line, inside, :] = jnp.where(keep_rows(direction, line), normed, 0.0)
            inverse[direction, here, :] = jnp.broadcast_to(norm, (line_len, channels))
            scaled[direction, here, :] = ratio

        def one_line(line, carry):
            here = rows(line, line_len)
            inputs = masked[direction, line, inside, :]
            hidden = taps_ref[direction, 0:1, :] * inputs
            for tap in range(1, taps):
                offset = offsets[tap]
                weight = taps_ref[direction, tap : tap + 1, :]
                size = abs(offset)
                if size < EDGE:
                    near = masked[direction, line, pl.ds(EDGE + offset, line_len), :]
                    hidden = hidden + weight * near
                elif offset > 0:
                    inner = hidden[: line_len - size] + weight * inputs[size:]
                    hidden = jnp.concatenate([inner, hidden[line_len - size :]], axis=0)
                else:
                    inner = hidden[size:] + weight * inputs[: line_len - size]
                    hidden = jnp.concatenate([hidden[:size], inner], axis=0)
            gate = 0.5 * jnp.tanh(0.5 * hidden) + 0.5
            activated[direction, here, :] = (hidden * gate).astype(BF16)
            slope[direction, here, :] = gate * (1.0 + hidden * (1.0 - gate))
            return carry

        lax.fori_loop(0, lines, one_line, 0)
        mixed = jnp.dot(activated[direction], mix_ref[direction], preferred_element_type=F32)
        return (stream[...] + mixed.astype(BF16).astype(F32)).astype(BF16)

    own_fields.wait()
    stream[...] = take(0, 0, arriving)
    cot_arriving, own_cot = enter(1, cotangent, 2)
    moved = forward(0)
    arriving = hand_over(2, 0, moved, 1)
    tables(1)
    stream[...] = take(2, 1, arriving)
    moved = forward(1)
    arriving = hand_over(3, 1, moved, 1)
    tables(2)
    stream[...] = take(3, 2, arriving)
    moved = forward(2)
    out_arriving, own_out = leave(4, 2, moved, imitated)
    own_cot.wait()
    grads[...] = take(1, 2, cot_arriving)

    def backward(direction):
        back = lax.dot_general(
            grads[...].astype(BF16),
            mix_ref[direction],
            (((1,), (1,)), ((), ())),
            preferred_element_type=F32,
        )
        for line in range(lines):
            here = pl.ds(line * line_len, line_len)
            local = back[line * line_len : (line + 1) * line_len] * slope[direction, here, :]
            padded[direction, line, inside, :] = local.astype(BF16).astype(F32)

        def one_line(line, carry):
            grad = padded[direction, line, inside, :]
            total = taps_ref[direction, 0:1, :] * grad
            for tap in range(1, taps):
                offset = -offsets[tap]
                weight = taps_ref[direction, tap : tap + 1, :]
                size = abs(offset)
                if size < EDGE:
                    near = padded[direction, line, pl.ds(EDGE + offset, line_len), :]
                    total = total + weight * near
                elif offset > 0:
                    inner = total[: line_len - size] + weight * grad[size:]
                    total = jnp.concatenate([inner, total[line_len - size :]], axis=0)
                else:
                    inner = total[size:] + weight * grad[: line_len - size]
                    total = jnp.concatenate([total[:size], inner], axis=0)
            stream[rows(line, line_len), :] = total
            return carry

        lax.fori_loop(0, lines, one_line, 0)
        out = []
        gains = jnp.zeros((8, channels), F32)
        for line in range(lines):
            here = pl.ds(line * line_len, line_len)
            total = jnp.where(keep_rows(direction, line), stream[here, :], 0.0)
            cell = total.astype(BF16).astype(F32)
            ratio = scaled[direction, here, :]
            gains = gains + fold(cell * ratio)
            weighted = cell * gain_ref[direction : direction + 1, :]
            centre = jnp.mean(weighted * ratio, axis=-1, keepdims=True)
            change = inverse[direction, here, :] * (weighted - ratio * centre)
            out.append((grads[here, :] + change).astype(BF16))
        sums[8 * taps : 8 * taps + 8, :] = gains
        return jnp.concatenate(out, axis=0)

    def tap_sums(direction):
        sums[0 : 8 * taps, :] = jnp.zeros((8 * taps, channels), F32)

        def one_line(line, carry):
            grad = padded[direction, line, inside, :]
            inputs = masked[direction, line, inside, :]
            for tap in range(taps):
                offset = -offsets[tap]
                size = abs(offset)
                slot = pl.ds(8 * tap, 8)
                if size == 0:
                    term = grad * inputs
                elif size < EDGE:
                    term = padded[direction, line, pl.ds(EDGE + offset, line_len), :] * inputs
                elif offset > 0:
                    term = grad[size:] * inputs[: line_len - size]
                else:
                    term = grad[: line_len - size] * inputs[size:]
                sums[slot, :] += fold(term)
            return carry

        lax.fori_loop(0, lines, one_line, 0)

    def mix_line(direction, grad_mixed):
        parts[direction] = lax.dot_general(
            activated[direction], grad_mixed, (((0,), (0,)), ((), ())), preferred_element_type=F32
        ).astype(BF16)
        return [
            remote(
                parts.at[direction, rows(peer(step), piece)],
                a_recv.at[direction, step],
                a_send.at[direction, step],
                a_arrive.at[direction, step],
                {"line": peer(step)},
            )
            for step in range(1, ranks)
        ]

    def mix_dp(direction, copies_in):
        total = parts[direction, rows(me, piece), :].astype(F32)
        for step in range(1, ranks):
            copies_in[step - 1].wait_recv()
            total = total + a_recv[direction, step].astype(F32)
        b_recv[direction, my_dp] = total.astype(BF16)
        return [
            remote(
                b_recv.at[direction, my_dp],
                b_recv.at[direction, my_dp],
                b_send.at[direction, step],
                b_arrive.at[direction, step],
                {"dp": dp_peer(step)},
            )
            for step in range(1, copies)
        ]

    def mix_spread(direction, copies_in):
        for copy in copies_in:
            copy.wait_recv()
        total = b_recv[direction, 0].astype(F32)
        for index in range(1, copies):
            total = total + b_recv[direction, index].astype(F32)
        full[direction, rows(me, piece), :] = (total * scale).astype(BF16)
        return [
            remote(
                full.at[direction, rows(me, piece)],
                full.at[direction, rows(me, piece)],
                c_send.at[direction, step],
                c_arrive.at[direction, step],
                {"line": peer(step)},
            )
            for step in range(1, ranks)
        ]

    def mix_finish(direction, copies_in):
        for copy in copies_in:
            copy.wait_recv()
        mix_out[direction] = full[direction].astype(F32)

    def tail_line(direction):
        line_tails[direction, me] = jnp.sum(sums[...].reshape(taps + 1, 8, channels), axis=1)
        return [
            remote(
                line_tails.at[direction, me],
                line_tails.at[direction, me],
                t_send.at[direction, step],
                t_arrive.at[direction, step],
                {"line": peer(step)},
            )
            for step in range(1, ranks)
        ]

    def tail_dp(direction, copies_in):
        for copy in copies_in:
            copy.wait_recv()
        total = line_tails[direction, 0]
        for index in range(1, ranks):
            total = total + line_tails[direction, index]
        dp_tails[direction, my_dp] = total
        return [
            remote(
                dp_tails.at[direction, my_dp],
                dp_tails.at[direction, my_dp],
                u_send.at[direction, step],
                u_arrive.at[direction, step],
                {"dp": dp_peer(step)},
            )
            for step in range(1, copies)
        ]

    def tail_finish(direction, copies_in):
        for copy in copies_in:
            copy.wait_recv()
        total = dp_tails[direction, 0]
        for index in range(1, copies):
            total = total + dp_tails[direction, index]
        total = total * scale
        taps_out[direction] = total[:taps]
        gain_out[direction : direction + 1, :] = total[taps : taps + 1]

    moved = backward(2)
    arriving = hand_over(5, 2, moved, -1)
    a2 = mix_line(2, grads[...].astype(BF16))
    tap_sums(2)
    t2 = tail_line(2)
    grads[...] = take(5, 1, arriving)
    moved = backward(1)
    arriving = hand_over(6, 1, moved, -1)
    b2 = mix_dp(2, a2)
    a1 = mix_line(1, grads[...].astype(BF16))
    tap_sums(1)
    t1 = tail_line(1)
    u2 = tail_dp(2, t2)
    grads[...] = take(6, 0, arriving)
    a0 = mix_line(0, grads[...].astype(BF16))
    b1 = mix_dp(1, a1)
    moved = backward(0)
    b0 = mix_dp(0, a0)
    last_arriving, own_last = leave(7, 0, moved, field_grad)
    tap_sums(0)
    t0 = tail_line(0)
    c2 = mix_spread(2, b2)
    c1 = mix_spread(1, b1)
    u1 = tail_dp(1, t1)
    u0 = tail_dp(0, t0)
    c0 = mix_spread(0, b0)
    tail_finish(2, u2)
    mix_finish(2, c2)
    mix_finish(1, c1)
    tail_finish(1, u1)
    mix_finish(0, c0)
    tail_finish(0, u0)
    for copy in out_arriving + last_arriving:
        copy.wait_recv()
    own_out.wait()
    own_last.wait()
    for copy in unsent:
        copy.wait_send()


def write_out(*refs):
    half = (len(refs) - 1) // 2
    sem = refs[-1]
    moves = [
        pltpu.make_async_copy(refs[index], refs[half + index], sem.at[index])
        for index in range(half)
    ]
    for move in moves:
        move.start()
    for move in moves:
        move.wait()


def body(fields, cotangent, norm_gain, kernel, mix_weight, line_order, line_starts):
    ranks = lax.axis_size("line")
    copies = lax.axis_size("dp")
    batch, cells, channels = fields.shape
    assert batch == 1
    directions, taps = kernel.shape[:2]
    lines = line_starts.shape[1]
    line_len = cells // lines
    scale = float(copies * batch * ranks * cells) ** (-0.5)
    piece = channels // ranks
    stages = 2 * directions + 2
    vmem = pl.BlockSpec(memory_space=pltpu.VMEM)
    hbm = pl.BlockSpec(memory_space=pltpu.HBM)
    anywhere = pl.BlockSpec(memory_space=pl.ANY)
    wide = pltpu.VMEM((directions, cells, channels), F32)
    edged = pltpu.VMEM((directions, lines, line_len + 2 * EDGE, channels), F32)
    dma = pltpu.SemaphoreType.DMA
    outs = (
        jax.ShapeDtypeStruct(fields.shape, BF16),
        jax.ShapeDtypeStruct(fields.shape, BF16),
        jax.ShapeDtypeStruct((directions, channels, channels), F32),
        jax.ShapeDtypeStruct((directions, taps, channels), F32),
        jax.ShapeDtypeStruct((directions, channels), F32),
    )
    results = pl.pallas_call(
        functools.partial(kernel_body, (ranks, copies, line_len, scale)),
        out_shape=outs,
        in_specs=[hbm] * 7,
        out_specs=(anywhere, anywhere, vmem, vmem, vmem),
        scratch_shapes=[
            pltpu.VMEM(norm_gain.shape, F32),
            pltpu.VMEM(kernel.shape, F32),
            pltpu.VMEM(mix_weight.shape, BF16),
            pltpu.VMEM(line_order.shape, jnp.int32),
            pltpu.VMEM(line_starts.shape, jnp.int32),
            pltpu.VMEM((directions, cells, cells), BF16),
            pltpu.VMEM((directions, cells, cells), BF16),
            pltpu.VMEM((stages, cells, channels), BF16),
            pltpu.VMEM((stages, cells, channels), BF16),
            pltpu.VMEM((cells, channels), F32),
            wide,
            wide,
            edged,
            wide,
            pltpu.VMEM((directions, cells, channels), BF16),
            pltpu.VMEM((cells, channels), F32),
            edged,
            pltpu.VMEM(((taps + 1) * 8, channels), F32),
            pltpu.VMEM((directions, channels, channels), BF16),
            pltpu.VMEM((directions, ranks, piece, channels), BF16),
            pltpu.VMEM((directions, copies, piece, channels), BF16),
            pltpu.VMEM((directions, channels, channels), BF16),
            pltpu.VMEM((directions, ranks, taps + 1, channels), F32),
            pltpu.VMEM((directions, copies, taps + 1, channels), F32),
            dma((stages, ranks)),
            dma((stages, ranks)),
            dma((directions, ranks)),
            dma((directions, ranks)),
            dma((directions, copies)),
            dma((directions, copies)),
            dma((directions, ranks)),
            dma((directions, ranks)),
            dma((directions, ranks)),
            dma((directions, ranks)),
            dma((directions, copies)),
            dma((directions, copies)),
            dma((stages,)),
            dma((5,)),
        ],
        compiler_params=pltpu.CompilerParams(
            collective_id=0, has_side_effects=True, vmem_limit_bytes=60 * 1024 * 1024
        ),
        name="mesh_block",
    )(fields, cotangent, norm_gain, kernel, mix_weight, line_order, line_starts)
    return pl.pallas_call(
        write_out,
        out_shape=outs,
        in_specs=[anywhere] * 5,
        out_specs=(hbm,) * 5,
        scratch_shapes=[dma((5,))],
        compiler_params=pltpu.CompilerParams(vmem_limit_bytes=60 * 1024 * 1024),
        name="write_out",
    )(*results)


def solution(mesh):
    in_specs = (
        P("dp", "line", None),
        P("dp", "line", None),
        P(),
        P(),
        P(),
        P(None, "line"),
        P(None, "line"),
    )
    out_specs = (P("dp", "line", None), P("dp", "line", None), P(), P(), P())
    return jax.shard_map(body, mesh=mesh, in_specs=in_specs, out_specs=out_specs, check_vma=False)
```

time: 55 us -> 60.2 us (1.095)
  Pallas kernels: 45.3 us -> 59.4 us
  local copies, waits for them, and re-layouts: 8.66 us -> 0 us
    pallas_call x0 -> x1, Pallas kernels: none -> 15.8 us  [body(): pl.pallas_call(write_out, out_shape=outs, in_specs=[anywhere] * 5, out_sp...]
    unnamed x19 -> x0, local copies, waits for them, and re-layouts: 8.66 us -> none
    pallas_call x1, Pallas kernels: 45.3 us -> 43.6 us  [body(): pl.pallas_call(functools.partial(kernel_body, (ranks, copies, line_len, s...]
where the time goes in v2:
time: 60.2 us; the launch traced here: 60 us
  Pallas kernels  59.4 us (99%)
  between operations  0.64 us (1%)
    pallas_call x1, Pallas kernels, body(): pl.pallas_call(functools.partial(kernel_body, (ranks, copies, line_len, s...  43.6 us
    pallas_call x1, Pallas kernels, body(): pl.pallas_call(write_out, out_shape=outs, in_specs=[anywhere] * 5, out_sp...  15.8 us

profile of v2, /device:TPU:0, one launch (start us, length us, event | category | flops | bytes accessed | tf_op | source)
XLA Modules:
  0.0 60.0 jit_solution(7871663293354399407)
XLA Ops:
  0.6 43.6 %mesh_block.1 = (bf16[1,512,128]{2,1,0:T(8,128)(2,1)}, bf16[1,512,128]{2,1,0:T(8,128)(2,1)}, f32[3,128,128]{2,1,0:T(8,128)}, f32[3,15,128]{2,1,0:T(8,128)}, f32[3,128]{1,0:T(4,128)}) custom-call(bf16[1,512,128]{2,1,0:T(8,128)(2,1)} %fields.1, bf16[1,512,128]{2,1,0:T(8,128)(2,1)} %cotangent.1, f32[3,128]{1,0:T(4,128)} %gain_hbm.1, f32[3,15,128]{2,1,0:T(8,128)} %taps_hbm.1, ...), custom_call_target="tpu_custom_call" | custom-call | tf_op jit(solution)/shard_map/mesh_block/pallas_call | solution.py:524
  44.2 15.8 %write_out.1 = (bf16[1,512,128]{2,1,0:T(8,128)(2,1)}, bf16[1,512,128]{2,1,0:T(8,128)(2,1)}, f32[3,128,128]{2,1,0:T(8,128)}, f32[3,15,128]{2,1,0:T(8,128)}, f32[3,128]{1,0:T(4,128)}) custom-call(bf16[1,512,128]{2,1,0:T(8,128)(2,1)} %get-tuple-element.10.refs_0_, bf16[1,512,128]{2,1,0:T(8,128)(2,1)} %get-tuple-element.11.refs_1_, ...), custom_call_target="tpu_custom_call" | custom-call | tf_op jit(solution)/shard_map/write_out/pallas_call | solution.py:574

commit v3 on v2

--- a/solution.py
+++ b/solution.py
@@ -177,7 +177,7 @@
 
     def hand_over(stage, direction, values, sign):
         out = []
-        for anchor in list(range(1, ranks)) + [0]:
+        for anchor in sorted(range(1, ranks), key=lambda step: abs(2 * step - ranks)) + [0]:
             span = pl.ds(anchor * block, block)
             chunk = jnp.dot(
                 scatter[direction, span, :], values, preferred_element_type=F32
@@ -278,7 +278,7 @@
     own_cot.wait()
     grads[...] = take(1, 2, cot_arriving)
 
-    def backward(direction):
+    def backward(direction, between=None):
         back = lax.dot_general(
             grads[...].astype(BF16),
             mix_ref[direction],
@@ -310,6 +310,7 @@
             return carry
 
         lax.fori_loop(0, lines, one_line, 0)
+        started = between() if between else None
         out = []
         gains = jnp.zeros((8, channels), F32)
         for line in range(lines):
@@ -323,7 +324,7 @@
             change = inverse[direction, here, :] * (weighted - ratio * centre)
             out.append((grads[here, :] + change).astype(BF16))
         sums[8 * taps : 8 * taps + 8, :] = gains
-        return jnp.concatenate(out, axis=0)
+        return jnp.concatenate(out, axis=0), started
 
     def tap_sums(direction):
         sums[0 : 8 * taps, :] = jnp.zeros((8 * taps, channels), F32)
@@ -444,13 +445,13 @@
         taps_out[direction] = total[:taps]
         gain_out[direction : direction + 1, :] = total[taps : taps + 1]
 
-    moved = backward(2)
+    moved, _ = backward(2)
     arriving = hand_over(5, 2, moved, -1)
     a2 = mix_line(2, grads[...].astype(BF16))
     tap_sums(2)
     t2 = tail_line(2)
     grads[...] = take(5, 1, arriving)
-    moved = backward(1)
+    moved, _ = backward(1)
     arriving = hand_over(6, 1, moved, -1)
     b2 = mix_dp(2, a2)
     a1 = mix_line(1, grads[...].astype(BF16))
@@ -460,16 +461,15 @@
     grads[...] = take(6, 0, arriving)
     a0 = mix_line(0, grads[...].astype(BF16))
     b1 = mix_dp(1, a1)
-    moved = backward(0)
-    b0 = mix_dp(0, a0)
+    moved, b0 = backward(0, lambda: mix_dp(0, a0))
     last_arriving, own_last = leave(7, 0, moved, field_grad)
     tap_sums(0)
     t0 = tail_line(0)
+    u1 = tail_dp(1, t1)
     c2 = mix_spread(2, b2)
     c1 = mix_spread(1, b1)
-    u1 = tail_dp(1, t1)
+    c0 = mix_spread(0, b0)
     u0 = tail_dp(0, t0)
-    c0 = mix_spread(0, b0)
     tail_finish(2, u2)
     mix_finish(2, c2)
     mix_finish(1, c1)
@@ -485,15 +485,23 @@
 
 
 def write_out(*refs):
-    half = (len(refs) - 1) // 2
-    sem = refs[-1]
-    moves = [
-        pltpu.make_async_copy(refs[index], refs[half + index], sem.at[index])
-        for index in range(half)
+    count = (len(refs) - 2) // 3
+    sources, targets, held = refs[:count], refs[count : 2 * count], refs[2 * count : 3 * count]
+    in_sem, out_sem = refs[-2:]
+    into = [
+        pltpu.make_async_copy(sources[index], held[index], in_sem.at[index])
+        for index in range(count)
     ]
-    for move in moves:
+    out = [
+        pltpu.make_async_copy(held[index], targets[index], out_sem.at[index])
+        for index in range(count)
+    ]
+    for move in into:
         move.start()
-    for move in moves:
+    for index in range(count):
+        into[index].wait()
+        out[index].start()
+    for move in out:
         move.wait()
 
 
@@ -576,7 +584,7 @@
         out_shape=outs,
         in_specs=[anywhere] * 5,
         out_specs=(hbm,) * 5,
-        scratch_shapes=[dma((5,))],
+        scratch_shapes=[pltpu.VMEM(out.shape, out.dtype) for out in outs] + [dma((5,)), dma((5,))],
         compiler_params=pltpu.CompilerParams(vmem_limit_bytes=60 * 1024 * 1024),
         name="write_out",
     )(*results)

time: 60.2 us -> 47.2 us (0.78)
  Pallas kernels: 59.4 us -> 46.4 us
    pallas_call x1, Pallas kernels: 15.8 us -> 1.82 us  [body(): pl.pallas_call(write_out, out_shape=outs, in_specs=[anywhere] * 5, out_sp...]
    pallas_call x1, Pallas kernels: 43.6 us -> 44.5 us  [body(): pl.pallas_call(functools.partial(kernel_body, (ranks, copies, line_len, s...]
where the time goes in v3:
time: 47.2 us; the launch traced here: 47 us
  Pallas kernels  46.4 us (98%)
  between operations  0.64 us (1%)
    pallas_call x1, Pallas kernels, body(): pl.pallas_call(functools.partial(kernel_body, (ranks, copies, line_len, s...  44.5 us
    pallas_call x1, Pallas kernels, body(): pl.pallas_call(write_out, out_shape=outs, in_specs=[anywhere] * 5, out_sp...  1.82 us

profile of v3, /device:TPU:0, one launch (start us, length us, event | category | flops | bytes accessed | tf_op | source)
XLA Modules:
  0.0 47.0 jit_solution(16176116705733840275)
XLA Ops:
  0.6 44.5 %mesh_block.1 = (bf16[1,512,128]{2,1,0:T(8,128)(2,1)}, bf16[1,512,128]{2,1,0:T(8,128)(2,1)}, f32[3,128,128]{2,1,0:T(8,128)}, f32[3,15,128]{2,1,0:T(8,128)}, f32[3,128]{1,0:T(4,128)}) custom-call(bf16[1,512,128]{2,1,0:T(8,128)(2,1)} %fields.1, bf16[1,512,128]{2,1,0:T(8,128)(2,1)} %cotangent.1, f32[3,128]{1,0:T(4,128)} %gain_hbm.1, f32[3,15,128]{2,1,0:T(8,128)} %taps_hbm.1, ...), custom_call_target="tpu_custom_call" | custom-call | tf_op jit(solution)/shard_map/mesh_block/pallas_call | solution.py:532
  45.2 1.8 %write_out.1 = (bf16[1,512,128]{2,1,0:T(8,128)(2,1)}, bf16[1,512,128]{2,1,0:T(8,128)(2,1)}, f32[3,128,128]{2,1,0:T(8,128)}, f32[3,15,128]{2,1,0:T(8,128)}, f32[3,128]{1,0:T(4,128)}) custom-call(bf16[1,512,128]{2,1,0:T(8,128)(2,1)} %get-tuple-element.10.refs_0_, bf16[1,512,128]{2,1,0:T(8,128)(2,1)} %get-tuple-element.11.refs_1_, ...), custom_call_target="tpu_custom_call" | custom-call | tf_op jit(solution)/shard_map/write_out/pallas_call | solution.py:582

commit v4 on v3

--- a/solution.py
+++ b/solution.py
@@ -83,7 +83,7 @@
     block = cells // ranks
     taps = taps_ref.shape[1]
     offsets = tap_offsets(taps)
-    piece = parts.shape[1] // ranks
+    piece = channels // ranks
     me = lax.axis_index("line")
     my_dp = lax.axis_index("dp")
 
@@ -158,16 +158,23 @@
     arriving, own_fields = enter(0, fields, 0)
 
     def tables(direction):
-        row = order_ref[direction : direction + 1, :]
         lanes = 128
-        across = lax.broadcasted_iota(jnp.int32, (cells, cells), 0)
-        scatter[direction] = jnp.where(across == row, 1.0, 0.0).astype(BF16)
-        turned = jnp.transpose(jnp.broadcast_to(row, (lanes, cells)))
-        for first in range(0, cells, lanes):
-            width = lax.broadcasted_iota(jnp.int32, (cells, lanes), 1) + first
-            gather[direction, :, first : first + lanes] = jnp.where(
-                turned == width, 1.0, 0.0
-            ).astype(BF16)
+
+        def one_part(part, carry):
+            span = rows(part, lanes)
+            across = lax.broadcasted_iota(jnp.int32, (lanes, cells), 0) + part * lanes
+            row = order_ref[direction : direction + 1, :]
+            scatter[direction, span, :] = jnp.where(across == row, 1.0, 0.0).astype(BF16)
+            some = order_ref[direction : direction + 1, span]
+            turned = jnp.transpose(jnp.broadcast_to(some, (lanes, lanes)))
+            for first in range(0, cells, lanes):
+                width = lax.broadcasted_iota(jnp.int32, (lanes, lanes), 1) + first
+                gather[direction, span, first : first + lanes] = jnp.where(
+                    turned == width, 1.0, 0.0
+                ).astype(BF16)
+            return carry
+
+        lax.fori_loop(0, cells // lanes, one_part, 0)
 
     masked[...] = jnp.zeros_like(masked)
     padded[...] = jnp.zeros_like(padded)
@@ -349,131 +356,148 @@
 
         lax.fori_loop(0, lines, one_line, 0)
 
-    def mix_line(direction, grad_mixed):
-        parts[direction] = lax.dot_general(
+    directions = parts.shape[1]
+    spans = (pl.ds(0, 1), pl.ds(1, directions - 1))
+
+    def mix_part(direction, grad_mixed):
+        part = lax.dot_general(
             activated[direction], grad_mixed, (((0,), (0,)), ((), ())), preferred_element_type=F32
         ).astype(BF16)
+        for rank in range(ranks):
+            parts[rank, direction] = part[rank * piece : (rank + 1) * piece]
+
+    def mix_line(group):
         return [
             remote(
-                parts.at[direction, rows(peer(step), piece)],
-                a_recv.at[direction, step],
-                a_send.at[direction, step],
-                a_arrive.at[direction, step],
+                parts.at[peer(step), spans[group]],
+                a_recv.at[step, spans[group]],
+                a_send.at[group, step],
+                a_arrive.at[group, step],
                 {"line": peer(step)},
             )
             for step in range(1, ranks)
         ]
 
-    def mix_dp(direction, copies_in):
-        total = parts[direction, rows(me, piece), :].astype(F32)
+    def mix_dp(group, copies_in):
+        span = spans[group]
+        total = parts[me, span].astype(F32)
         for step in range(1, ranks):
             copies_in[step - 1].wait_recv()
-            total = total + a_recv[direction, step].astype(F32)
-        b_recv[direction, my_dp] = total.astype(BF16)
+            total = total + a_recv[step, span].astype(F32)
+        b_recv[my_dp, span] = total.astype(BF16)
         return [
             remote(
-                b_recv.at[direction, my_dp],
-                b_recv.at[direction, my_dp],
-                b_send.at[direction, step],
-                b_arrive.at[direction, step],
+                b_recv.at[my_dp, span],
+                b_recv.at[my_dp, span],
+                b_send.at[group, step],
+                b_arrive.at[group, step],
                 {"dp": dp_peer(step)},
             )
             for step in range(1, copies)
         ]
 
-    def mix_spread(direction, copies_in):
+    def mix_spread(group, copies_in):
+        span = spans[group]
         for copy in copies_in:
             copy.wait_recv()
-        total = b_recv[direction, 0].astype(F32)
+        total = b_recv[0, span].astype(F32)
         for index in range(1, copies):
-            total = total + b_recv[direction, index].astype(F32)
-        full[direction, rows(me, piece), :] = (total * scale).astype(BF16)
+            total = total + b_recv[index, span].astype(F32)
+        full[me, span] = (total * scale).astype(BF16)
         return [
             remote(
-                full.at[direction, rows(me, piece)],
-                full.at[direction, rows(me, piece)],
-                c_send.at[direction, step],
-                c_arrive.at[direction, step],
+                full.at[me, span],
+                full.at[me, span],
+                c_send.at[group, step],
+                c_arrive.at[group, step],
                 {"line": peer(step)},
             )
             for step in range(1, ranks)
         ]
 
-    def mix_finish(direction, copies_in):
+    def mix_finish(group, copies_in):
         for copy in copies_in:
             copy.wait_recv()
-        mix_out[direction] = full[direction].astype(F32)
-
-    def tail_line(direction):
-        line_tails[direction, me] = jnp.sum(sums[...].reshape(taps + 1, 8, channels), axis=1)
+        for direction in range(group, directions if group else 1):
+            for rank in range(ranks):
+                mix_out[direction, rank * piece : (rank + 1) * piece, :] = full[
+                    rank, direction
+                ].astype(F32)
+
+    def tail_part(direction):
+        line_tails[me, direction] = jnp.sum(sums[...].reshape(taps + 1, 8, channels), axis=1)
+
+    def tail_line(group):
+        span = spans[group]
         return [
             remote(
-                line_tails.at[direction, me],
-                line_tails.at[direction, me],
-                t_send.at[direction, step],
-                t_arrive.at[direction, step],
+                line_tails.at[me, span],
+                line_tails.at[me, span],
+                t_send.at[group, step],
+                t_arrive.at[group, step],
                 {"line": peer(step)},
             )
             for step in range(1, ranks)
         ]
 
-    def tail_dp(direction, copies_in):
+    def tail_dp(group, copies_in):
+        span = spans[group]
         for copy in copies_in:
             copy.wait_recv()
-        total = line_tails[direction, 0]
+        total = line_tails[0, span]
         for index in range(1, ranks):
-            total = total + line_tails[direction, index]
-        dp_tails[direction, my_dp] = total
+            total = total + line_tails[index, span]
+        dp_tails[my_dp, span] = total
         return [
             remote(
-                dp_tails.at[direction, my_dp],
-                dp_tails.at[direction, my_dp],
-                u_send.at[direction, step],
-                u_arrive.at[direction, step],
+                dp_tails.at[my_dp, span],
+                dp_tails.at[my_dp, span],
+                u_send.at[group, step],
+                u_arrive.at[group, step],
                 {"dp": dp_peer(step)},
             )
             for step in range(1, copies)
         ]
 
-    def tail_finish(direction, copies_in):
+    def tail_finish(group, copies_in):
         for copy in copies_in:
             copy.wait_recv()
-        total = dp_tails[direction, 0]
-        for index in range(1, copies):
-            total = total + dp_tails[direction, index]
-        total = total * scale
-        taps_out[direction] = total[:taps]
-        gain_out[direction : direction + 1, :] = total[taps : taps + 1]
+        for direction in range(group, directions if group else 1):
+            total = dp_tails[0, direction]
+            for index in range(1, copies):
+                total = total + dp_tails[index, direction]
+            total = total * scale
+            taps_out[direction] = total[:taps]
+            gain_out[direction : direction + 1, :] = total[taps : taps + 1]
 
     moved, _ = backward(2)
     arriving = hand_over(5, 2, moved, -1)
-    a2 = mix_line(2, grads[...].astype(BF16))
+    mix_part(2, grads[...].astype(BF16))
     tap_sums(2)
-    t2 = tail_line(2)
+    tail_part(2)
     grads[...] = take(5, 1, arriving)
     moved, _ = backward(1)
     arriving = hand_over(6, 1, moved, -1)
-    b2 = mix_dp(2, a2)
-    a1 = mix_line(1, grads[...].astype(BF16))
+    mix_part(1, grads[...].astype(BF16))
+    a1 = mix_line(1)
     tap_sums(1)
+    tail_part(1)
     t1 = tail_line(1)
-    u2 = tail_dp(2, t2)
+    b1 = mix_dp(1, a1)
     grads[...] = take(6, 0, arriving)
-    a0 = mix_line(0, grads[...].astype(BF16))
-    b1 = mix_dp(1, a1)
+    mix_part(0, grads[...].astype(BF16))
+    a0 = mix_line(0)
+    u1 = tail_dp(1, t1)
     moved, b0 = backward(0, lambda: mix_dp(0, a0))
     last_arriving, own_last = leave(7, 0, moved, field_grad)
     tap_sums(0)
+    tail_part(0)
     t0 = tail_line(0)
-    u1 = tail_dp(1, t1)
-    c2 = mix_spread(2, b2)
     c1 = mix_spread(1, b1)
     c0 = mix_spread(0, b0)
     u0 = tail_dp(0, t0)
-    tail_finish(2, u2)
-    mix_finish(2, c2)
+    tail_finish(1, u1)
     mix_finish(1, c1)
-    tail_finish(1, u1)
     mix_finish(0, c0)
     tail_finish(0, u0)
     for copy in out_arriving + last_arriving:
@@ -553,24 +577,24 @@
             pltpu.VMEM((cells, channels), F32),
             edged,
             pltpu.VMEM(((taps + 1) * 8, channels), F32),
-            pltpu.VMEM((directions, channels, channels), BF16),
-            pltpu.VMEM((directions, ranks, piece, channels), BF16),
-            pltpu.VMEM((directions, copies, piece, channels), BF16),
-            pltpu.VMEM((directions, channels, channels), BF16),
-            pltpu.VMEM((directions, ranks, taps + 1, channels), F32),
-            pltpu.VMEM((directions, copies, taps + 1, channels), F32),
+            pltpu.VMEM((ranks, directions, piece, channels), BF16),
+            pltpu.VMEM((ranks, directions, piece, channels), BF16),
+            pltpu.VMEM((copies, directions, piece, channels), BF16),
+            pltpu.VMEM((ranks, directions, piece, channels), BF16),
+            pltpu.VMEM((ranks, directions, taps + 1, channels), F32),
+            pltpu.VMEM((copies, directions, taps + 1, channels), F32),
             dma((stages, ranks)),
             dma((stages, ranks)),
-            dma((directions, ranks)),
-            dma((directions, ranks)),
-            dma((directions, copies)),
-            dma((directions, copies)),
-            dma((directions, ranks)),
-            dma((directions, ranks)),
-            dma((directions, ranks)),
-            dma((directions, ranks)),
-            dma((directions, copies)),
-            dma((directions, copies)),
+            dma((2, ranks)),
+            dma((2, ranks)),
+            dma((2, copies)),
+            dma((2, copies)),
+            dma((2, ranks)),
+            dma((2, ranks)),
+            dma((2, ranks)),
+            dma((2, ranks)),
+            dma((2, copies)),
+            dma((2, copies)),
             dma((stages,)),
             dma((5,)),
         ],

time: 47.2 us -> 49.2 us (1.042)
  Pallas kernels: 46.4 us -> 48.3 us
    pallas_call x1, Pallas kernels: 44.5 us -> 46.5 us  [body(): pl.pallas_call(functools.partial(kernel_body, (ranks, copies, line_len, s...]
where the time goes in v4:
time: 49.2 us; the launch traced here: 49 us
  Pallas kernels  48.3 us (98%)
  between operations  0.64 us (1%)
    pallas_call x1, Pallas kernels, body(): pl.pallas_call(functools.partial(kernel_body, (ranks, copies, line_len, s...  46.5 us
    pallas_call x1, Pallas kernels, body(): pl.pallas_call(write_out, out_shape=outs, in_specs=[anywhere] * 5, out_sp...  1.82 us

profile of v4, /device:TPU:0, one launch (start us, length us, event | category | flops | bytes accessed | tf_op | source)
XLA Modules:
  0.0 49.0 jit_solution(10580217775284171179)
XLA Ops:
  0.6 46.5 %mesh_block.1 = (bf16[1,512,128]{2,1,0:T(8,128)(2,1)}, bf16[1,512,128]{2,1,0:T(8,128)(2,1)}, f32[3,128,128]{2,1,0:T(8,128)}, f32[3,15,128]{2,1,0:T(8,128)}, f32[3,128]{1,0:T(4,128)}) custom-call(bf16[1,512,128]{2,1,0:T(8,128)(2,1)} %fields.1, bf16[1,512,128]{2,1,0:T(8,128)(2,1)} %cotangent.1, f32[3,128]{1,0:T(4,128)} %gain_hbm.1, f32[3,15,128]{2,1,0:T(8,128)} %taps_hbm.1, ...), custom_call_target="tpu_custom_call" | custom-call | tf_op jit(solution)/shard_map/mesh_block/pallas_call | solution.py:556
  47.1 1.8 %write_out.1 = (bf16[1,512,128]{2,1,0:T(8,128)(2,1)}, bf16[1,512,128]{2,1,0:T(8,128)(2,1)}, f32[3,128,128]{2,1,0:T(8,128)}, f32[3,15,128]{2,1,0:T(8,128)}, f32[3,128]{1,0:T(4,128)}) custom-call(bf16[1,512,128]{2,1,0:T(8,128)(2,1)} %get-tuple-element.10.refs_0_, bf16[1,512,128]{2,1,0:T(8,128)(2,1)} %get-tuple-element.11.refs_1_, ...), custom_call_target="tpu_custom_call" | custom-call | tf_op jit(solution)/shard_map/write_out/pallas_call | solution.py:606

commit v5 on v3

--- a/solution.py
+++ b/solution.py
@@ -177,7 +177,7 @@
 
     def hand_over(stage, direction, values, sign):
         out = []
-        for anchor in sorted(range(1, ranks), key=lambda step: abs(2 * step - ranks)) + [0]:
+        for anchor in list(range(1, ranks)) + [0]:
             span = pl.ds(anchor * block, block)
             chunk = jnp.dot(
                 scatter[direction, span, :], values, preferred_element_type=F32
@@ -278,7 +278,7 @@
     own_cot.wait()
     grads[...] = take(1, 2, cot_arriving)
 
-    def backward(direction, between=None):
+    def backward(direction):
         back = lax.dot_general(
             grads[...].astype(BF16),
             mix_ref[direction],
@@ -310,7 +310,6 @@
             return carry
 
         lax.fori_loop(0, lines, one_line, 0)
-        started = between() if between else None
         out = []
         gains = jnp.zeros((8, channels), F32)
         for line in range(lines):
@@ -324,7 +323,7 @@
             change = inverse[direction, here, :] * (weighted - ratio * centre)
             out.append((grads[here, :] + change).astype(BF16))
         sums[8 * taps : 8 * taps + 8, :] = gains
-        return jnp.concatenate(out, axis=0), started
+        return jnp.concatenate(out, axis=0)
 
     def tap_sums(direction):
         sums[0 : 8 * taps, :] = jnp.zeros((8 * taps, channels), F32)
@@ -445,13 +444,13 @@
         taps_out[direction] = total[:taps]
         gain_out[direction : direction + 1, :] = total[taps : taps + 1]
 
-    moved, _ = backward(2)
+    moved = backward(2)
     arriving = hand_over(5, 2, moved, -1)
     a2 = mix_line(2, grads[...].astype(BF16))
     tap_sums(2)
     t2 = tail_line(2)
     grads[...] = take(5, 1, arriving)
-    moved, _ = backward(1)
+    moved = backward(1)
     arriving = hand_over(6, 1, moved, -1)
     b2 = mix_dp(2, a2)
     a1 = mix_line(1, grads[...].astype(BF16))
@@ -461,15 +460,16 @@
     grads[...] = take(6, 0, arriving)
     a0 = mix_line(0, grads[...].astype(BF16))
     b1 = mix_dp(1, a1)
-    moved, b0 = backward(0, lambda: mix_dp(0, a0))
+    moved = backward(0)
+    b0 = mix_dp(0, a0)
     last_arriving, own_last = leave(7, 0, moved, field_grad)
     tap_sums(0)
     t0 = tail_line(0)
-    u1 = tail_dp(1, t1)
     c2 = mix_spread(2, b2)
     c1 = mix_spread(1, b1)
+    u1 = tail_dp(1, t1)
+    u0 = tail_dp(0, t0)
     c0 = mix_spread(0, b0)
-    u0 = tail_dp(0, t0)
     tail_finish(2, u2)
     mix_finish(2, c2)
     mix_finish(1, c1)

time: 47.2 us -> 46.2 us (0.979)
  Pallas kernels: 46.4 us -> 45.4 us
    pallas_call x1, Pallas kernels: 44.5 us -> 43.6 us  [body(): pl.pallas_call(functools.partial(kernel_body, (ranks, copies, line_len, s...]
where the time goes in v5:
time: 46.2 us; the launch traced here: 46 us
  Pallas kernels  45.4 us (98%)
  between operations  0.64 us (1%)
    pallas_call x1, Pallas kernels, body(): pl.pallas_call(functools.partial(kernel_body, (ranks, copies, line_len, s...  43.6 us
    pallas_call x1, Pallas kernels, body(): pl.pallas_call(write_out, out_shape=outs, in_specs=[anywhere] * 5, out_sp...  1.82 us

profile of v5, /device:TPU:0, one launch (start us, length us, event | category | flops | bytes accessed | tf_op | source)
XLA Modules:
  0.0 46.0 jit_solution(13367624979672953994)
XLA Ops:
  0.6 43.6 %mesh_block.1 = (bf16[1,512,128]{2,1,0:T(8,128)(2,1)}, bf16[1,512,128]{2,1,0:T(8,128)(2,1)}, f32[3,128,128]{2,1,0:T(8,128)}, f32[3,15,128]{2,1,0:T(8,128)}, f32[3,128]{1,0:T(4,128)}) custom-call(bf16[1,512,128]{2,1,0:T(8,128)(2,1)} %fields.1, bf16[1,512,128]{2,1,0:T(8,128)(2,1)} %cotangent.1, f32[3,128]{1,0:T(4,128)} %gain_hbm.1, f32[3,15,128]{2,1,0:T(8,128)} %taps_hbm.1, ...), custom_call_target="tpu_custom_call" | custom-call | tf_op jit(solution)/shard_map/mesh_block/pallas_call | solution.py:532
  44.2 1.8 %write_out.1 = (bf16[1,512,128]{2,1,0:T(8,128)(2,1)}, bf16[1,512,128]{2,1,0:T(8,128)(2,1)}, f32[3,128,128]{2,1,0:T(8,128)}, f32[3,15,128]{2,1,0:T(8,128)}, f32[3,128]{1,0:T(4,128)}) custom-call(bf16[1,512,128]{2,1,0:T(8,128)(2,1)} %get-tuple-element.10.refs_0_, bf16[1,512,128]{2,1,0:T(8,128)(2,1)} %get-tuple-element.11.refs_1_, ...), custom_call_target="tpu_custom_call" | custom-call | tf_op jit(solution)/shard_map/write_out/pallas_call | solution.py:582

commit v6 on v5

--- a/solution.py
+++ b/solution.py
@@ -258,7 +258,7 @@
             slope[direction, here, :] = gate * (1.0 + hidden * (1.0 - gate))
             return carry
 
-        lax.fori_loop(0, lines, one_line, 0)
+        lax.fori_loop(0, lines, one_line, 0, unroll=True)
         mixed = jnp.dot(activated[direction], mix_ref[direction], preferred_element_type=F32)
         return (stream[...] + mixed.astype(BF16).astype(F32)).astype(BF16)
 
@@ -309,7 +309,7 @@
             stream[rows(line, line_len), :] = total
             return carry
 
-        lax.fori_loop(0, lines, one_line, 0)
+        lax.fori_loop(0, lines, one_line, 0, unroll=True)
         out = []
         gains = jnp.zeros((8, channels), F32)
         for line in range(lines):

time: 46.2 us -> 45.8 us (level)
  Pallas kernels: 45.4 us -> 44.9 us
where the time goes in v6:
time: 45.8 us; the launch traced here: 45.6 us
  Pallas kernels  44.9 us (98%)
  between operations  0.64 us (1%)
    pallas_call x1, Pallas kernels, body(): pl.pallas_call(functools.partial(kernel_body, (ranks, copies, line_len, s...  43.1 us
    pallas_call x1, Pallas kernels, body(): pl.pallas_call(write_out, out_shape=outs, in_specs=[anywhere] * 5, out_sp...  1.82 us

profile of v6, /device:TPU:0, one launch (start us, length us, event | category | flops | bytes accessed | tf_op | source)
XLA Modules:
  0.0 45.6 jit_solution(13694965500236375464)
XLA Ops:
  0.6 43.1 %mesh_block.1 = (bf16[1,512,128]{2,1,0:T(8,128)(2,1)}, bf16[1,512,128]{2,1,0:T(8,128)(2,1)}, f32[3,128,128]{2,1,0:T(8,128)}, f32[3,15,128]{2,1,0:T(8,128)}, f32[3,128]{1,0:T(4,128)}) custom-call(bf16[1,512,128]{2,1,0:T(8,128)(2,1)} %fields.1, bf16[1,512,128]{2,1,0:T(8,128)(2,1)} %cotangent.1, f32[3,128]{1,0:T(4,128)} %gain_hbm.1, f32[3,15,128]{2,1,0:T(8,128)} %taps_hbm.1, ...), custom_call_target="tpu_custom_call" | custom-call | tf_op jit(solution)/shard_map/mesh_block/pallas_call | solution.py:532
  43.7 1.8 %write_out.1 = (bf16[1,512,128]{2,1,0:T(8,128)(2,1)}, bf16[1,512,128]{2,1,0:T(8,128)(2,1)}, f32[3,128,128]{2,1,0:T(8,128)}, f32[3,15,128]{2,1,0:T(8,128)}, f32[3,128]{1,0:T(4,128)}) custom-call(bf16[1,512,128]{2,1,0:T(8,128)(2,1)} %get-tuple-element.10.refs_0_, bf16[1,512,128]{2,1,0:T(8,128)(2,1)} %get-tuple-element.11.refs_1_, ...), custom_call_target="tpu_custom_call" | custom-call | tf_op jit(solution)/shard_map/write_out/pallas_call | solution.py:582
